TPU v7x, 32 devices: a whole 2x2x4 slice. The times are simulated.
32 devices in a mesh: grp: 2 (over y), row: 4 (over z), col: 4 (over x, core).
Axes of the slice: x: 2, y: 2, z: 4, core: 2. Of those that a mesh axis runs over, the one named last changes fastest.
Arguments:
- root_covariance: float32 [40, 4, 128, 20, 4, 128], P('grp', 'col', None, None, 'row'), parts along dimension 0, as said below
- factor_one: float32 [40, 4, 128, 512], P('grp', 'row', None, 'col'), parts along dimension 0, may hold values from -0.18 to 0.18
- inverse_one: float32 [1024, 512], P(('grp', 'col')), parts along dimension 0, as said below
- pattern_one: int32 [160], P('grp'), parts along dimension 0, may hold values from 0 to 1, as said below
- factor_parent: float32 [1024, 512], P(('grp', 'row'), 'col'), parts along dimension 0, may hold values from -0.18 to 0.18
- factor_root: float32 [40, 4, 128, 512], P('grp', 'row', None, 'col'), parts along dimension 0, may hold values from -0.18 to 0.18
- inverse_two: float32 [1024, 512], P(('grp', 'col')), parts along dimension 0, as said below
- pattern_two: int32 [160], P('grp'), parts along dimension 0, may hold values from 0 to 1, as said below
Outputs:
- sigma_cross_one: float32 [1024, 20, 4, 128], P(('grp', 'row'), None, 'col'), parts along dimension 0
- sigma_block_one: float32 [1024, 512], P(('grp', 'col'), 'row'), parts along dimension 0
- sigma_parent_two: float32 [1024, 512], P(('grp', 'row')), parts along dimension 0
- sigma_cross_two: float32 [1024, 20, 4, 128], P(('grp', 'row'), None, 'col'), parts along dimension 0
- sigma_block_two: float32 [1024, 512], P(('grp', 'col'), 'row'), parts along dimension 0
There are 2 independent parts, one for each index of `grp`. A program takes and returns all parts, laid end to end along the dimension named above; each array names one. Nothing has to cross between parts.
Inputs may be any that keep to these rules, and one draw needn't show every extreme that they name: `root_covariance`: symmetric and positive definite. `inverse_one`: lower triangular with a positive diagonal. `inverse_two`: lower triangular with a positive diagonal. `pattern_one`: 1 marks a root block in the row structure. `pattern_two`: 1 only where pattern_one is 1.
All inputs are finite; a program needn't handle non-finite values.
Results may differ from a plain program's by a relative error of at most 0.0001.
Values sent between devices are 32-bit elements; how exact they have to be, the bound alone decides.
No kernel may reach another device: no remote copies, remote signals or barrier semaphores. Data moves between devices by JAX's collectives and lax.ppermute only.
A program may use at most 256 MiB of HBM per device.

v0:
```python
import jax
import jax.numpy as jnp
from jax import lax
from jax.sharding import PartitionSpec as P

B = 128


def broadcast(block, axis, owner):
    block = jnp.where(lax.axis_index(axis) == owner, block, jnp.zeros_like(block))
    return lax.psum(block, axis)


def matmul(left_side, right_side):
    return jnp.dot(
        left_side, right_side, precision=lax.Precision.HIGHEST, preferred_element_type=jnp.float32
    )


def contract_lead(left_side, right_side):
    return lax.dot_general(
        left_side,
        right_side,
        (((0,), (0,)), ((), ())),
        precision=lax.Precision.HIGHEST,
        preferred_element_type=jnp.float32,
    )


def contract_pair(left_side, right_side):
    return lax.dot_general(
        left_side,
        right_side,
        (((0,), (1,)), ((), ())),
        precision=lax.Precision.HIGHEST,
        preferred_element_type=jnp.float32,
    )


def local_mask(pattern, position, grid_size):
    table = pattern.reshape(-1, grid_size)
    picked = jnp.sum(jnp.where(jnp.arange(grid_size)[None, :] == position, table, 0), axis=1)
    return jnp.repeat(picked.astype(jnp.float32), B)


def panel_solve(lower_rows, inverse):
    return lax.psum(matmul(lower_rows, inverse), "col")


def from_diagonal(row_block):
    return broadcast(row_block, "row", lax.axis_index("col"))


def cross_reduce(term_pairs):
    running_sum = None
    for solved_rows, y_block, leading in term_pairs:
        if leading:
            addend = contract_lead(solved_rows, y_block)
        else:
            addend = contract_pair(solved_rows, y_block)
        running_sum = addend if running_sum is None else running_sum + addend
    return lax.psum_scatter(running_sum, "row", scatter_dimension=0, tiled=True)


def sigma_reduce(term_pairs, inverse, position, column_share):
    own_columns = lax.dynamic_slice_in_dim(inverse, position * column_share, column_share, 1)
    running_sum = contract_lead(inverse, own_columns)
    for solved_cols, y_block, leading in term_pairs:
        if leading:
            running_sum = running_sum + contract_lead(solved_cols, y_block)
        else:
            running_sum = running_sum + contract_pair(solved_cols, y_block)
    return lax.psum_scatter(running_sum, "col", scatter_dimension=0, tiled=True)


def local(
    root_covariance,
    factor_one,
    inverse_one,
    pattern_one,
    factor_parent,
    factor_root,
    inverse_two,
    pattern_two,
):
    grid_size = lax.axis_size("row")
    row_position = lax.axis_index("row")
    col_position = lax.axis_index("col")
    covariance = root_covariance.reshape(
        root_covariance.shape[0] * root_covariance.shape[2],
        root_covariance.shape[3] * root_covariance.shape[5],
    )
    column_share = inverse_one.shape[1] // grid_size
    local_rows = covariance.shape[0]
    row_mask_one = local_mask(pattern_one, row_position, grid_size)
    col_mask_one = local_mask(pattern_one, col_position, grid_size)
    lower_one = factor_one.reshape(-1, factor_one.shape[3]) * row_mask_one[:, None]
    solved_rows_one = panel_solve(lower_one, inverse_one)
    solved_cols_one = from_diagonal(solved_rows_one)
    image_one = cross_reduce(((solved_rows_one, covariance, False),))
    cross_one = -image_one * col_mask_one[None, :]
    block_one = sigma_reduce(
        ((solved_cols_one, image_one, False),), inverse_one, row_position, column_share
    )
    row_mask_two = local_mask(pattern_two, row_position, grid_size)
    col_mask_two = local_mask(pattern_two, col_position, grid_size)
    lower_two = jnp.concatenate(
        [factor_parent, factor_root.reshape(-1, factor_root.shape[3]) * row_mask_two[:, None]], 0
    )
    solved_rows_two = panel_solve(lower_two, inverse_two)
    solved_cols_two = from_diagonal(solved_rows_two)
    rows_parent = solved_rows_two[:column_share]
    rows_root = solved_rows_two[column_share:]
    cols_parent = solved_cols_two[:column_share]
    cols_root = solved_cols_two[column_share:]
    parent_term = contract_lead(block_one, cols_parent) + matmul(cross_one, cols_root)
    image_parent = lax.psum(parent_term, "col")
    parent_cols = from_diagonal(image_parent)
    parent_slice = lax.dynamic_slice_in_dim(
        parent_cols, row_position * column_share, column_share, 1
    )
    image_root = cross_reduce(((rows_root, covariance, False), (rows_parent, cross_one, True)))
    cross_two = -image_root * col_mask_two[None, :]
    block_two = sigma_reduce(
        ((cols_root, image_root, False), (cols_parent, parent_slice, True)),
        inverse_two,
        row_position,
        column_share,
    )
    cross_one_out = cross_one.reshape(column_share, local_rows // B, 1, B)
    cross_two_out = cross_two.reshape(column_share, local_rows // B, 1, B)
    return (cross_one_out, block_one, -image_parent, cross_two_out, block_two)


def solution(mesh):
    return jax.shard_map(
        local,
        mesh=mesh,
        in_specs=(
            P("grp", "col", None, None, "row", None),
            P("grp", "row", None, "col"),
            P(("grp", "col"), None),
            P("grp"),
            P(("grp", "row"), "col"),
            P("grp", "row", None, "col"),
            P(("grp", "col"), None),
            P("grp"),
        ),
        out_specs=(
            P(("grp", "row"), None, "col", None),
            P(("grp", "col"), "row"),
            P(("grp", "row"), None),
            P(("grp", "row"), None, "col", None),
            P(("grp", "col"), "row"),
        ),
        check_vma=False,
    )
```

profile of v0, /device:TPU:14, one launch (start us, length us, event | category | flops | bytes accessed | tf_op | source)
XLA Modules:
  0.0 1071.6 jit_solution(5882242278262034705)
XLA Ops:
  9.1 1.7 bitcast_multiply_fusion
  10.9 1.7 bitcast_multiply_fusion.1
  12.6 5.9 fusion.36
  18.5 6.2 fusion.11
  24.8 202.8 %reduce = f32[20,128,20,128]{3,2,1,0:T(8,128)} reduce(f32[20,1,128,20,1,128]{5,4,3,2,1,0:T(1,128)} %param.8, f32[]{:T(128)} %constant.20), dimensions={1,4}, to_apply=%param.8.reduce_sub_computation | reduce | bytes 52428804 | tf_op args[0]
  227.6 88.3 %fusion.2 = f32[512,2560]{1,0:T(8,128)} fusion(f32[2560,512]{1,0:T(8,128)} %get-tuple-element.21, f32[320,8,20,128]{3,2,1,0:T(8,128)} %bitcast.37), kind=kOutput, calls=%fused_computation.2 | convolution fusion | flops 40265318400 | bytes 36700160 | tf_op jit(solution)/shard_map/dot_general | solution.py:31
  316.0 3.3 broadcast_select_fusion.1
  320.4 3.2 broadcast_select_fusion
  324.2 86.8 %reduce-scatter.5.cloned.1.call-done = f32[128,2560]{1,0:T(8,128)} async-done(((f32[512,2560]{1,0:T(8,128)}), f32[128,2560]{1,0:T(8,128)}) %reduce-scatter.5.cloned.1.call-update) | async-done | bytes 1310736 | tf_op jit(solution)/shard_map/reduce_scatter | solution.py:62
  411.0 368.8 %all-reduce.13.cloned.1.call-done = (f32[2560,512]{1,0:T(8,128)}, f32[2688,512]{1,0:T(8,128)}) async-done(((f32[2560,512]{1,0:T(8,128)}, f32[2688,512]{1,0:T(8,128)}), (f32[2560,512]{1,0:T(8,128)}, f32[2688,512]{1,0:T(8,128)})) %all-reduce.13.cloned.1.call-update) | async-done | bytes 10747920 | tf_op jit(solution)/shard_map/psum | solution.py:11
  779.8 6.6 convolution_add_fusion.1
  786.6 20.0 %reduce-scatter.7.cloned.1.call-done = f32[128,128]{0,1:T(8,128)} async-done(((f32[512,128]{0,1:T(8,128)}), f32[128,128]{0,1:T(8,128)}) %reduce-scatter.7.cloned.1.call-update) | async-done | bytes 65552 | tf_op jit(solution)/shard_map/reduce_scatter | solution.py:73
  808.0 6.2 fusion.15
  814.2 88.1 %fusion = f32[512,2560]{1,0:T(8,128)} fusion(f32[320,8,20,128]{3,2,1,0:T(8,128)} %bitcast.38, f32[2688,512]{1,0:T(8,128)} %get-tuple-element.22), kind=kOutput, calls=%fused_computation | convolution fusion | flops 40265318400 | bytes 41943040 | tf_op jit(solution)/shard_map/dot_general | solution.py:31
  902.4 1.8 broadcast_select_fusion.2
  904.3 7.8 convolution_add_fusion
  913.1 2.0 copy.25
  915.9 24.7 %all-reduce.9.cloned.1.call-done = f32[128,512]{1,0:T(8,128)} async-done(((f32[128,512]{1,0:T(8,128)}), f32[128,512]{1,0:T(8,128)}) %all-reduce.9.cloned.1.call-update) | async-done | bytes 262160 | tf_op jit(solution)/shard_map/psum | solution.py:11
  940.5 1.4 fusion.25
  941.9 94.6 %reduce-scatter.9.cloned.1.call-done = f32[128,2560]{1,0:T(8,128)} async-done(((f32[512,2560]{1,0:T(8,128)}), f32[128,2560]{1,0:T(8,128)}) %reduce-scatter.9.cloned.1.call-update) | async-done | bytes 1310736 | tf_op jit(solution)/shard_map/reduce_scatter | solution.py:62
  1036.5 6.7 fusion.21
  1043.8 2.0 copy.27
  1045.8 17.2 %reduce-scatter.11.cloned.1.call-done = f32[128,128]{0,1:T(8,128)} async-done(((f32[512,128]{0,1:T(8,128)}), f32[128,128]{0,1:T(8,128)}) %reduce-scatter.11.cloned.1.call-update) | async-done | bytes 65552 | tf_op jit(solution)/shard_map/reduce_scatter | solution.py:73
  1063.0 1.6 copy.28
  (55 shorter events, 7.6 us)
Async XLA Ops:
  7.2 11.4 %copy-start = (f32[128,512]{1,0:T(8,128)S(1)}, f32[128,512]{1,0:T(8,128)}, u32[]{:S(2)}) copy-start(f32[128,512]{1,0:T(8,128)} %param.14) | copy-start | bytes 786436
  7.2 5.4 copy-start.3
  7.2 220.4 %all-reduce.11.cloned.1.call-start = ((), (), s32[]{:S(2)}) async-start(), calls=%async_computation.10 | async-start | bytes 21495808 | tf_op jit(solution)/shard_map/psum | solution.py:47
  10.8 7.7 copy-start.5
  24.7 386.2 %reduce-scatter.5.cloned.1.call-start = ((), (), s32[]{:S(2)}) async-start(), calls=%async_computation.4 | async-start | bytes 6553600 | tf_op jit(solution)/shard_map/reduce_scatter | solution.py:62
  315.9 3.4 slice-start
  316.0 463.8 %all-reduce.13.cloned.1.call-start = ((), (), s32[]{:S(2)}) async-start(), calls=%async_computation.11 | async-start | bytes 21495808 | tf_op jit(solution)/shard_map/psum | solution.py:11
  316.0 4.4 slice-start.1
  323.6 483.0 %reduce-scatter.7.cloned.1.call-start = ((), (), s32[]{:S(2)}) async-start(), calls=%async_computation.5 | async-start | bytes 327680 | tf_op jit(solution)/shard_map/reduce_scatter | solution.py:73
  411.0 375.5 %copy-start.1 = (f32[128,2560]{1,0:T(8,128)S(1)}, f32[128,2560]{1,0:T(8,128)}, u32[]{:S(2)}) copy-start(f32[128,2560]{1,0:T(8,128)} %reduce-scatter.5.cloned.1.call-done) | copy-start | bytes 3932164
  786.4 116.0 %all-reduce.7.cloned.1.call-start = ((), (), s32[]{:S(2)}) async-start(), calls=%async_computation.6 | async-start | bytes 524288 | tf_op jit(solution)/shard_map/psum | solution.py:117
  814.2 126.3 %all-reduce.9.cloned.1.call-start = ((), (), s32[]{:S(2)}) async-start(), calls=%async_computation.8 | async-start | bytes 524288 | tf_op jit(solution)/shard_map/psum | solution.py:11
  904.2 132.3 %reduce-scatter.9.cloned.1.call-start = ((), (), s32[]{:S(2)}) async-start(), calls=%async_computation.7 | async-start | bytes 6553600 | tf_op jit(solution)/shard_map/reduce_scatter | solution.py:62
  912.1 3.0 copy-start.4
  912.1 150.9 %reduce-scatter.11.cloned.1.call-start = ((), (), s32[]{:S(2)}) async-start(), calls=%async_computation.9 | async-start | bytes 327680 | tf_op jit(solution)/shard_map/reduce_scatter | solution.py:73
  1036.5 6.7 copy-start.2
Sparse Core Ops, SparseCore 0:
  24.9 191.6 all-reduce.10
  316.1 94.8 reduce-scatter.4
  413.6 366.1 all-reduce.12
  786.5 20.0 reduce-scatter.6
  814.3 31.8 all-reduce.6
  904.3 36.1 all-reduce.8
  942.9 93.5 reduce-scatter.8
  1043.3 19.6 reduce-scatter.10
where the time goes:
time: 1080 us; the launch traced here: 1070 us
  waiting for transfers between devices  612 us (57%)
  matrix products  219 us (20%)
  other arithmetic  215 us (20%)
  between operations  14.6 us (1%)
    psum x2, waiting for transfers between devices, broadcast(): return lax.psum(block, axis)  393 us
    unnamed x2, other arithmetic  203 us
    dot_general x4, matrix products, contract_pair(): lax.dot_general(left_side, right_side, (((0,), (1,)), ((), ())), precisio...  190 us
    reduce_scatter x2, waiting for transfers between devices, cross_reduce(): return lax.psum_scatter(running_sum, 'row', scatter_dimension=0, tiled=True)  181 us
    reduce_scatter x2, waiting for transfers between devices, sigma_reduce(): return lax.psum_scatter(running_sum, 'col', scatter_dimension=0, tiled=True)  37.2 us
  transfers between devices with their start and end apart: 8, of which 6 were waited for; matrix products, arithmetic and copies ran while one was open for 29% of the time, Pallas kernels for 0%

commit v1 on v0

v1 whole, which is shorter than its diff:
```python
import functools

import jax
import jax.numpy as jnp
from jax import lax
from jax.experimental import pallas as pl
from jax.experimental.pallas import tpu as pltpu
from jax.sharding import PartitionSpec as P

B = 128
VMEM_LIMIT = 52 * 1024 * 1024
VMEM = pl.BlockSpec(memory_space=pltpu.VMEM)
SMEM = pl.BlockSpec(memory_space=pltpu.SMEM)


def split(values):
    high = values.astype(jnp.bfloat16)
    low = (values - high.astype(jnp.float32)).astype(jnp.bfloat16)
    return high, low


def lanes_dot(left, right):
    return lax.dot_general(
        left, right, (((1,), (1,)), ((), ())), preferred_element_type=jnp.float32
    )


def plain_dot(left, right):
    return lax.dot_general(
        left, right, (((1,), (0,)), ((), ())), preferred_element_type=jnp.float32
    )


def three_products(dot, left, right):
    left_high, left_low = left
    right_high, right_low = right
    rows = left_high.shape[0]
    both = dot(jnp.concatenate([left_high, left_low], 0), right_high)
    return both[:rows] + both[rows:] + dot(left_high, right_low)


def stacked(high, low):
    return jnp.concatenate([high, low], 0)


def call(kernel, name, out_shape, operands, flops, in_specs=None, scratch=()):
    size = sum(a.size * a.dtype.itemsize for a in operands)
    size += sum(a.size * a.dtype.itemsize for a in jax.tree.leaves(out_shape))
    return pl.pallas_call(
        kernel,
        name=name,
        out_shape=out_shape,
        in_specs=in_specs or [VMEM] * len(operands),
        out_specs=jax.tree.map(lambda _: VMEM, out_shape),
        scratch_shapes=scratch,
        compiler_params=pltpu.CompilerParams(vmem_limit_bytes=VMEM_LIMIT),
        cost_estimate=pl.CostEstimate(flops=flops, bytes_accessed=size, transcendentals=0),
    )(*operands)


def shape_of(shape, dtype=jnp.float32):
    return jax.ShapeDtypeStruct(shape, dtype)


def active_order(pattern_one, pattern_two, position, grid_size, capacity):
    mine = (jnp.arange(grid_size) == position)[None, :]
    one = jnp.sum(jnp.where(mine, pattern_one.reshape(-1, grid_size), 0), axis=1)
    two = jnp.sum(jnp.where(mine, pattern_two.reshape(-1, grid_size), 0), axis=1)
    key = one + two
    index = jnp.arange(key.shape[0])
    ahead = (key[None, :] > key[:, None]) | (
        (key[None, :] == key[:, None]) & (index[None, :] < index[:, None])
    )
    rank = jnp.sum(ahead.astype(jnp.int32), axis=1)
    slots = jnp.arange(capacity)
    order = jnp.sum(jnp.where(rank[None, :] == slots[:, None], index[None, :], 0), axis=1)
    return order.astype(jnp.int32), jnp.sum(one), jnp.sum(two)


def pack_kernel(cap_one, cap_two, order, counts, f_one, inv_one, f_par, f_root, inv_two, out_one, out_two):
    width = inv_one.shape[1]
    for i in range(cap_one):
        out_one[pl.ds(i * B, B), :] = jnp.where(i < counts[0], f_one[order[i]], 0.0)
    out_one[pl.ds(cap_one * B, width), :] = inv_one[...].T
    for i in range(cap_two):
        out_two[pl.ds(i * B, B), :] = jnp.where(i < counts[1], f_root[order[i]], 0.0)
    out_two[pl.ds(cap_two * B, width), :] = inv_two[...].T
    out_two[pl.ds(cap_two * B + width, f_par.shape[0]), :] = f_par[...]


def joined(ref, start, size):
    return jnp.concatenate([ref[k, pl.ds(start, size), :] for k in range(ref.shape[0])], 1)


def solve_one_kernel(cap, gathered, out):
    width = out.shape[0] // 2
    inverse = split(joined(gathered, cap * B, width))

    def step(i, carry):
        start = pl.multiple_of(i * 2 * B, 2 * B)
        rows = split(joined(gathered, start, 2 * B))
        high, low = split(three_products(lanes_dot, inverse, rows))
        out[:width, pl.ds(start, 2 * B)] = high
        out[width:, pl.ds(start, 2 * B)] = low
        return carry

    lax.fori_loop(0, cap // 2, step, 0)


def parent_kernel(cap_two, gathered, out):
    width, share = out.shape
    inverse = split(joined(gathered, cap_two * B, width))
    parent = split(joined(gathered, cap_two * B + width, share))
    out[...] = three_products(lanes_dot, inverse, parent)


def solve_two_kernel(
    cap_one, cap_two, place, gathered_one, gathered_two, parents,
    out_full, out_root, out_lead, out_diag_one, out_diag_two,
    weight_high, weight_low,
):
    grid_size, width, share = parents.shape
    row, col = place[0], place[1]
    for k in range(grid_size):
        total = jnp.zeros((width, share), jnp.float32)
        for m in range(grid_size):
            piece = gathered_one[k, pl.ds(cap_one * B + m * share, share), :]
            total = total + three_products(plain_dot, split(parents[m]), split(piece))
        high, low = split(total)
        weight_high[:, k * share:(k + 1) * share] = high
        weight_low[:, k * share:(k + 1) * share] = low
    weight = (weight_high[...], weight_low[...])
    row_start = cap_one * B + pl.multiple_of(row * share, share)
    col_start = cap_one * B + pl.multiple_of(col * share, share)
    inv_row = split(joined(gathered_one, row_start, share))
    inv_col = split(joined(gathered_one, col_start, share))
    out_lead[...] = three_products(lanes_dot, inv_row, weight)
    out_diag_one[...] = three_products(lanes_dot, inv_col, inv_row)
    row_start = cap_two * B + pl.multiple_of(row * share, share)
    col_start = cap_two * B + pl.multiple_of(col * share, share)
    inv_row = split(joined(gathered_two, row_start, share))
    inv_col = split(joined(gathered_two, col_start, share))
    out_diag_two[...] = three_products(lanes_dot, inv_col, inv_row)
    inverse = split(joined(gathered_two, cap_two * B, width))

    def both(i, carry):
        start = pl.multiple_of(i * 2 * B, 2 * B)
        own = three_products(lanes_dot, inverse, split(joined(gathered_two, start, 2 * B)))
        high, low = split(own)
        out_root[:width, pl.ds(start, 2 * B)] = high
        out_root[width:, pl.ds(start, 2 * B)] = low
        other = three_products(lanes_dot, weight, split(joined(gathered_one, start, 2 * B)))
        high, low = split(own - other)
        out_full[:width, pl.ds(start, 2 * B)] = high
        out_full[width:, pl.ds(start, 2 * B)] = low
        return carry

    def first_only(i, carry):
        start = pl.multiple_of(i * 2 * B, 2 * B)
        other = three_products(lanes_dot, weight, split(joined(gathered_one, start, 2 * B)))
        high, low = split(-other)
        out_full[:width, pl.ds(start, 2 * B)] = high
        out_full[width:, pl.ds(start, 2 * B)] = low
        return carry

    lax.fori_loop(0, cap_two // 2, both, 0)
    lax.fori_loop(cap_two // 2, cap_one // 2, first_only, 0)


def image_kernel(
    blocks, cap, chunk, order_in, order_out, counts, solved, cov_a, cov_b, out, high, low, total
):
    step = pl.program_id(0)
    width = out.shape[0]
    total[...] = jnp.zeros_like(total)

    @pl.when(2 * step < counts[1])
    def _():
        for lead in range(0, cap, chunk):
            size = min(chunk, cap - lead)

            @pl.when(lead < counts[0])
            def _():
                for j in range(size):
                    for half, cov in enumerate((cov_a, cov_b)):
                        piece = cov[pl.ds(order_in[lead + j], B, stride=blocks), :]
                        piece_high, piece_low = split(piece)
                        high[half * B:(half + 1) * B, j * B:(j + 1) * B] = piece_high
                        low[half * B:(half + 1) * B, j * B:(j + 1) * B] = piece_low
                span = slice(lead * B, (lead + size) * B)
                both = lanes_dot(solved[:, span], high[:, :size * B])
                more = lanes_dot(solved[:width, span], low[:, :size * B])
                total[...] += both[:width] + both[width:] + more

    out[...] = total[...]


def image(covariance, solved, order_in, order_out, counts, cap_out, name):
    width = solved.shape[0] // 2
    cap_in = solved.shape[1] // B
    rows, blocks = covariance.shape[0], covariance.shape[1]
    flat = covariance.reshape(rows * blocks, B)
    chunk = 4

    def place(which):
        def index_map(i, order_in, order_out, counts):
            last = jnp.maximum(counts[1] - 1, 0)
            return (order_out[jnp.minimum(2 * i + which, last)], 0)

        return pl.BlockSpec((B * blocks, B), index_map)

    grid_spec = pltpu.PrefetchScalarGridSpec(
        num_scalar_prefetch=3,
        grid=(cap_out // 2,),
        in_specs=[
            pl.BlockSpec(solved.shape, lambda i, *_: (0, 0), pipeline_mode=pl.Buffered(1)),
            place(0),
            place(1),
        ],
        out_specs=pl.BlockSpec((width, 2 * B), lambda i, *_: (0, i)),
        scratch_shapes=[
            pltpu.VMEM((2 * B, chunk * B), jnp.bfloat16),
            pltpu.VMEM((2 * B, chunk * B), jnp.bfloat16),
            pltpu.VMEM((width, 2 * B), jnp.float32),
        ],
    )
    return pl.pallas_call(
        functools.partial(image_kernel, blocks, cap_in, chunk),
        name=name,
        grid_spec=grid_spec,
        out_shape=shape_of((width, cap_out * B)),
        compiler_params=pltpu.CompilerParams(vmem_limit_bytes=VMEM_LIMIT),
        cost_estimate=pl.CostEstimate(
            flops=6 * width * cap_in * B * cap_out * B,
            bytes_accessed=4 * cap_out * B * blocks * B + 8 * width * cap_out * B,
            transcendentals=0,
        ),
    )(order_in, order_out, counts, solved, flat, flat)


def unpack_kernel(blocks, cap, which, order, counts, packed, out):
    share = packed.shape[0]
    out[...] = jnp.zeros_like(out)
    for i in range(min(cap, blocks)):

        @pl.when(i < counts[which])
        def _():
            out[pl.ds(order[i], share, stride=blocks), :] = -packed[:, i * B:(i + 1) * B]


def unpack(packed, order, counts, which, blocks, name):
    share, cap = packed.shape[0], packed.shape[1] // B
    flat = call(
        functools.partial(unpack_kernel, blocks, cap, which),
        name,
        shape_of((share * blocks, B)),
        (order, counts, packed),
        1,
        in_specs=[SMEM, SMEM, VMEM],
    )
    return flat.reshape(share, blocks, 1, B)


def gram_one_kernel(image_rows, solved_one, solved_two, out):
    grid_size, _, share = out.shape
    width = solved_one.shape[0] // 2
    rows = split(image_rows[...])
    for half, solved in enumerate((solved_one, solved_two)):
        product = three_products(lanes_dot, rows, (solved[:width, :], solved[width:, :]))
        for k in range(grid_size):
            out[k, half * share:(half + 1) * share, :] = product[:, k * share:(k + 1) * share]


def gram_two_kernel(image_rows, solved_root, image_parent, parent, out):
    grid_size, share, _ = out.shape
    width = solved_root.shape[0] // 2
    rows = split(image_rows[...])
    product = three_products(lanes_dot, rows, (solved_root[:width, :], solved_root[width:, :]))
    product = product + three_products(
        lanes_dot, split(image_parent[...].T), split(parent[...])
    )
    for k in range(grid_size):
        out[k, :, :] = product[:, k * share:(k + 1) * share]


def swap_grid(block, grid_size):
    pairs = [
        (r * grid_size + c, c * grid_size + r) for r in range(grid_size) for c in range(grid_size)
    ]
    return lax.ppermute(block, ("row", "col"), pairs)


def scatter_sum(pieces, grid_size, position):
    total = lax.dynamic_index_in_dim(pieces, position, 0, keepdims=False)
    for shift in range(1, grid_size):
        target = lax.rem(position + shift, grid_size)
        piece = lax.dynamic_index_in_dim(pieces, target, 0, keepdims=False)
        total = total + lax.ppermute(
            piece, "row", [(i, (i + shift) % grid_size) for i in range(grid_size)]
        )
    return total


def gather_rows(block, grid_size, position):
    gathered = jnp.zeros((grid_size,) + block.shape, block.dtype)
    gathered = lax.dynamic_update_index_in_dim(gathered, block, position, 0)
    for shift in range(1, grid_size):
        other = lax.ppermute(block, "row", [(i, (i + shift) % grid_size) for i in range(grid_size)])
        source = lax.rem(position + grid_size - shift, grid_size)
        gathered = lax.dynamic_update_index_in_dim(gathered, other, source, 0)
    return gathered


def run(
    cap_one, cap_two, root_covariance, factor_one, inverse_one, pattern_one,
    factor_parent, factor_root, inverse_two, pattern_two,
):
    grid_size = lax.axis_size("row")
    row = lax.axis_index("row")
    col = lax.axis_index("col")
    share, width = inverse_one.shape
    blocks = root_covariance.shape[3]
    covariance = root_covariance.reshape(-1, blocks, B)
    row_order, row_one, row_two = active_order(pattern_one, pattern_two, row, grid_size, cap_one)
    col_order, col_one, col_two = active_order(pattern_one, pattern_two, col, grid_size, cap_one)
    place = jnp.stack([row, col]).astype(jnp.int32)
    row_counts = jnp.stack([row_one, row_two])
    col_counts = jnp.stack([col_one, col_two])

    packed_one, packed_two = call(
        functools.partial(pack_kernel, cap_one, cap_two),
        "pack",
        (shape_of((cap_one * B + width, share)), shape_of((cap_two * B + width + share, share))),
        (
            row_order, row_counts, factor_one.reshape(blocks, B, share), inverse_one,
            factor_parent, factor_root.reshape(blocks, B, share), inverse_two,
        ),
        1,
        in_specs=[SMEM, SMEM] + [VMEM] * 5,
    )
    gathered_one = lax.all_gather(packed_one, "col")
    gathered_two = lax.all_gather(packed_two, "col")

    solved_one = call(
        functools.partial(solve_one_kernel, cap_one),
        "solve_one",
        shape_of((2 * width, cap_one * B), jnp.bfloat16),
        (gathered_one,),
        6 * width * width * cap_one * B,
    )
    counts = jnp.stack([row_one, col_one])
    image_one = image(covariance, solved_one, row_order, col_order, counts, cap_one, "image_one")
    image_one = lax.psum_scatter(image_one, "row", scatter_dimension=0, tiled=True)

    parent = call(
        functools.partial(parent_kernel, cap_two),
        "parent",
        shape_of((width, share)),
        (gathered_two,),
        6 * width * width * share,
    )
    parents = gather_rows(parent, grid_size, row)
    solved_two, solved_root, lead, diag_one, diag_two = call(
        functools.partial(solve_two_kernel, cap_one, cap_two),
        "solve_two",
        (
            shape_of((2 * width, cap_one * B), jnp.bfloat16),
            shape_of((2 * width, cap_two * B), jnp.bfloat16),
            shape_of((share, width)),
            shape_of((share, share)),
            shape_of((share, share)),
        ),
        (place, gathered_one, gathered_two, parents),
        6 * width * width * (cap_one + cap_two) * B,
        in_specs=[SMEM] + [VMEM] * 3,
        scratch=[pltpu.VMEM((width, width), jnp.bfloat16)] * 2,
    )
    counts = jnp.stack([row_one, col_two])
    image_two = image(covariance, solved_two, row_order, col_order, counts, cap_two, "image_two")
    image_two = lax.psum_scatter(image_two, "row", scatter_dimension=0, tiled=True)

    rows_one = swap_grid(image_one, grid_size)
    cross_one = unpack(image_one, col_order, col_counts, 0, blocks, "cross_one")
    gram_one = call(
        gram_one_kernel,
        "gram_one",
        shape_of((grid_size, 2 * share, share)),
        (rows_one, solved_one, solved_two),
        12 * share * width * cap_one * B,
    )
    gram_one = scatter_sum(gram_one, grid_size, row)
    block_one = gram_one[:share] + diag_one
    mixed = swap_grid(gram_one[share:], grid_size)
    own_lead = lax.dynamic_slice_in_dim(lead, col * share, share, 1)
    mixed_all = lax.all_gather(mixed, "col")
    parent_out = jnp.concatenate([mixed_all[k] for k in range(grid_size)], 1) - lead

    rows_two = swap_grid(image_two, grid_size)
    cross_two = unpack(image_two, col_order, col_counts, 1, blocks, "cross_two")
    gram_two = call(
        gram_two_kernel,
        "gram_two",
        shape_of((grid_size, share, share)),
        (rows_two, solved_root, own_lead - mixed, parent),
        6 * share * width * cap_two * B,
    )
    block_two = scatter_sum(gram_two, grid_size, row) + diag_two
    return cross_one, block_one, parent_out, cross_two, block_two


def local(*arguments):
    blocks = arguments[0].shape[3]
    full = blocks + blocks % 2
    return run(full, full, *arguments)


def solution(mesh):
    return jax.shard_map(
        local,
        mesh=mesh,
        in_specs=(
            P("grp", "col", None, None, "row", None),
            P("grp", "row", None, "col"),
            P(("grp", "col"), None),
            P("grp"),
            P(("grp", "row"), "col"),
            P("grp", "row", None, "col"),
            P(("grp", "col"), None),
            P("grp"),
        ),
        out_specs=(
            P(("grp", "row"), None, "col", None),
            P(("grp", "col"), "row"),
            P(("grp", "row"), None),
            P(("grp", "row"), None, "col", None),
            P(("grp", "col"), "row"),
        ),
        check_vma=False,
    )
```

time: 1080 us -> 485 us (0.45)
  waiting for transfers between devices: 612 us -> 322 us
  matrix products: 219 us -> 0 us
  other arithmetic: 215 us -> 10.8 us
  Pallas kernels: 0 us -> 97.7 us
  starting transfers between devices: 0.33 us -> 23.5 us
    psum x4 -> x0, waiting for transfers between devices: 394 us -> none  [the longest x2 393 us: broadcast(): return lax.psum(block, axis)]
    dot_general x12 -> x0, matrix products: 219 us -> none  [the longest x4 190 us: contract_pair(): lax.dot_general(left_side, right_side, (((0,), (1,)), ((), ())), precisio...]
    unnamed x2 -> x0, other arithmetic: 203 us -> none
    pallas_call x0 -> x10, Pallas kernels: none -> 97.7 us  [the longest x8 55.1 us: call(): pl.pallas_call(kernel, name=name, out_shape=out_shape, in_specs=in_specs...]
    ppermute x0 -> x12, waiting for transfers between devices: none -> 95.2 us  [the longest x3 50.4 us: gather_rows(): lax.ppermute(block, 'row', [(i, (i + shift) % grid_size) for i in range(g...]
    all_gather x0 -> x2, waiting for transfers between devices: none -> 57.3 us  [the longest x1 44.3 us: run(): gathered_one = lax.all_gather(packed_one, 'col')]
    reduce_scatter x4 -> x2, waiting for transfers between devices: 219 us -> 169 us  [the longest x1 154 us: run(): lax.psum_scatter(image_two, 'row', scatter_dimension=0, tiled=True)]
    ppermute x0 -> x12, starting transfers between devices: none -> 23.3 us  [the longest x3 10.2 us: swap_grid(): return lax.ppermute(block, ('row', 'col'), pairs)]
  transfers between devices with their start and end apart: 8 -> 16, of which waited for: 6 -> 11; matrix products, arithmetic and copies ran while one was open for 29% -> 2% of each run, Pallas kernels for 0% -> 19%
where the time goes in v1:
time: 485 us; the launch traced here: 482 us
  waiting for transfers between devices  322 us (66%)
  Pallas kernels  97.7 us (20%)
  starting transfers between devices  23.5 us (5%)
  between operations  14 us (3%)
  other arithmetic  10.8 us (2%)
  local copies, waits for them, and re-layouts  7.4 us (2%)
  blocking collectives  5.77 us (1%)
    reduce_scatter x1, waiting for transfers between devices, run(): lax.psum_scatter(image_two, 'row', scatter_dimension=0, tiled=True)  154 us
    pallas_call x8, Pallas kernels, call(): pl.pallas_call(kernel, name=name, out_shape=out_shape, in_specs=in_specs...  55.1 us
    ppermute x3, waiting for transfers between devices, gather_rows(): lax.ppermute(block, 'row', [(i, (i + shift) % grid_size) for i in range(g...  50.4 us
    ppermute x6, waiting for transfers between devices, scatter_sum(): lax.ppermute(piece, 'row', [(i, (i + shift) % grid_size) for i in range(g...  44.8 us
    all_gather x1, waiting for transfers between devices, run(): gathered_one = lax.all_gather(packed_one, 'col')  44.3 us
    pallas_call x2, Pallas kernels, image(): pl.pallas_call(functools.partial(image_kernel, blocks, cap_in, chunk), na...  42.6 us
    reduce_scatter x1, waiting for transfers between devices, run(): lax.psum_scatter(image_one, 'row', scatter_dimension=0, tiled=True)  15.5 us
    all_gather x1, waiting for transfers between devices, run(): gathered_two = lax.all_gather(packed_two, 'col')  13 us
  transfers between devices with their start and end apart: 16, of which 11 were waited for; matrix products, arithmetic and copies ran while one was open for 2% of the time, Pallas kernels for 19%

profile of v1, /device:TPU:14, one launch (start us, length us, event | category | flops | bytes accessed | tf_op | source)
XLA Modules:
  0.0 481.5 jit_solution(3737930785739237292)
XLA Ops:
  16.3 3.3 pack.1
  22.0 44.3 %all-gather.6.cloned.1.call-done = f32[12288,128]{1,0:T(8,128)} async-done(((f32[3072,128]{1,0:T(8,128)}), f32[12288,128]{1,0:T(8,128)}) %all-gather.6.cloned.1.call-update) | async-done | bytes 6291472 | tf_op jit(solution)/shard_map/all_gather | solution.py:341
  66.3 11.7 %solve_one.1.solved.solved_one = bf16[1024,2560]{1,0:T(8,128)(2,1)} custom-call(f32[4,3072,128]{2,1,0:T(8,128)} %bitcast.57), custom_call_target="tpu_custom_call" | custom-call | flops 4026531840 | bytes 11534336 | tf_op jit(solution)/shard_map/solve_one/pallas_call | solution.py:49
  77.9 23.3 %image_one.1 = f32[512,2560]{1,0:T(8,128)} custom-call(s32[20]{0:T(128)S(1)} %select_reduce_fusion.order.order_in, s32[20]{0:T(128)S(1)} %select_reduce_fusion.3.order_out.order, s32[2]{0:T(128)S(1)} %pad_add_fusion.1.counts, bf16[1024,2560]{1,0:T(8,128)(2,1)} %solve_one.1.solved.solved_one, f32[51200,128]{1,0:T(8,128)} %bitcast.53, f32[51200,128]{1,0:T(8,128)} %bitcast.54), custom_call_target="tpu_custom_call" | custom-call | flops 20132659200 | bytes 36700160 | tf_op jit(solution)/shard_map/image_one/pallas_call | solution.py:227
  102.7 13.0 %all-gather.8.cloned.1.call-done = f32[12800,128]{1,0:T(8,128)} async-done(((f32[3200,128]{1,0:T(8,128)}), f32[12800,128]{1,0:T(8,128)}) %all-gather.8.cloned.1.call-update) | async-done | bytes 6553616 | tf_op jit(solution)/shard_map/all_gather | solution.py:342
  115.7 3.4 parent.1
  123.8 6.7 %collective-permute-done.1 = f32[512,128]{1,0:T(8,128)S(1)} collective-permute-done((f32[512,128]{1,0:T(8,128)S(1)}, f32[512,128]{1,0:T(8,128)S(1)}, u32[]{:S(2)}, u32[]{:S(2)}) %collective-permute-start.1) | collective-permute-done | bytes 262176 | tf_op jit(solution)/shard_map/ppermute | solution.py:308
  130.6 31.3 %collective-permute-done.2 = f32[512,128]{1,0:T(8,128)S(1)} collective-permute-done((f32[512,128]{1,0:T(8,128)S(1)}, f32[512,128]{1,0:T(8,128)S(1)}, u32[]{:S(2)}, u32[]{:S(2)}) %collective-permute-start.2) | collective-permute-done | bytes 262176 | tf_op jit(solution)/shard_map/ppermute | solution.py:308
  161.9 12.3 %collective-permute-done.3 = f32[512,128]{1,0:T(8,128)S(1)} collective-permute-done((f32[512,128]{1,0:T(8,128)S(1)}, f32[512,128]{1,0:T(8,128)S(1)}, u32[]{:S(2)}, u32[]{:S(2)}) %collective-permute-start.3) | collective-permute-done | bytes 262176 | tf_op jit(solution)/shard_map/ppermute | solution.py:308
  174.3 21.4 %solve_two.1 = (bf16[1024,2560]{1,0:T(8,128)(2,1)}, bf16[1024,2560]{1,0:T(8,128)(2,1)}, f32[128,512]{1,0:T(8,128)S(1)}, f32[128,128]{1,0:T(8,128)S(1)}, f32[128,128]{1,0:T(8,128)S(1)}) custom-call(s32[2]{0:T(128)S(1)} %pad_add_fusion.3.place, f32[4,3072,128]{2,1,0:T(8,128)} %bitcast.58, f32[4,3200,128]{2,1,0:T(8,128)} %bitcast.49, ...), custom_call_target="tpu_custom_call" | custom-call | flops 8053063680 | bytes 24772616 | tf_op jit(solution)/shard_map/solve_two/pallas_call | solution.py:49
  196.4 19.3 %image_two.1 = f32[512,2560]{1,0:T(8,128)} custom-call(s32[20]{0:T(128)S(1)} %select_reduce_fusion.order.order_in, s32[20]{0:T(128)S(1)} %select_reduce_fusion.3.order_out.order, s32[2]{0:T(128)S(1)} %pad_add_fusion.4.counts, bf16[1024,2560]{1,0:T(8,128)(2,1)} %get-tuple-element.14.solved_two.solved, f32[51200,128]{1,0:T(8,128)} %bitcast.55, ...), custom_call_target="tpu_custom_call" | custom-call | flops 20132659200 | bytes 36700160 | tf_op jit(solution)/shard_map/image_two/pallas_call | solution.py:227
  215.7 15.5 %reduce-scatter.3.cloned.1.call-done.packed = f32[128,2560]{1,0:T(8,128)} async-done(((f32[512,2560]{1,0:T(8,128)}), f32[128,2560]{1,0:T(8,128)}) %reduce-scatter.3.cloned.1.call-update) | async-done | bytes 1310736 | tf_op jit(solution)/shard_map/reduce_scatter | solution.py:353
  231.2 3.1 collective-permute-start
  234.4 153.7 %reduce-scatter.5.cloned.1.call-done.packed = f32[128,2560]{1,0:T(8,128)} async-done(((f32[512,2560]{1,0:T(8,128)}), f32[128,2560]{1,0:T(8,128)}) %reduce-scatter.5.cloned.1.call-update) | async-done | bytes 1310736 | tf_op jit(solution)/shard_map/reduce_scatter | solution.py:380
  388.1 4.3 collective-permute-start.8
  392.4 7.2 %gram_one.1 = f32[4,256,128]{2,1,0:T(8,128)S(1)} custom-call(f32[128,2560]{1,0:T(8,128)S(1)} %collective-permute-done.image_rows, bf16[1024,2560]{1,0:T(8,128)(2,1)} %solve_one.1.solved.solved_one, bf16[1024,2560]{1,0:T(8,128)(2,1)} %get-tuple-element.14.solved_two.solved), custom_call_target="tpu_custom_call" | custom-call | flops 2013265920 | bytes 12320768 | tf_op jit(solution)/shard_map/gram_one/pallas_call | solution.py:49
  400.4 3.9 collective-permute-start.5
  404.3 39.2 %collective-permute-done.4 = f32[256,128]{1,0:T(8,128)} collective-permute-done((f32[256,128]{1,0:T(8,128)}, f32[256,128]{1,0:T(8,128)}, u32[]{:S(2)}, u32[]{:S(2)}) %collective-permute-start.4) | collective-permute-done | bytes 131104 | tf_op jit(solution)/shard_map/ppermute | solution.py:298
  446.6 2.8 collective-permute-start.7
  454.7 5.8 %all-gather.2 = f32[512,128]{1,0:T(8,128)S(1)} all-gather(f32[128,128]{1,0:T(8,128)S(1)} %collective-permute-done.7), channel_id=4, replica_groups=mesh['grp'=2,'row'=4,'col'=4] {'col'}, dimensions={0}, use_global_device_ids=true | all-gather | bytes 327680 | tf_op jit(solution)/shard_map/all_gather | solution.py:395
  460.5 4.2 gram_two.1
  464.8 2.5 collective-permute-start.10
  470.1 2.1 collective-permute-done.10
  472.2 2.1 collective-permute-done.11
  (72 shorter events, 31.0 us)
Async XLA Ops:
  7.2 59.1 %all-gather.6.cloned.1.call-start = ((), (), s32[]{:S(2)}) async-start(), calls=%async_computation.4 | async-start | bytes 7864320 | tf_op jit(solution)/shard_map/all_gather | solution.py:341
  12.2 1.3 copy-start
  13.5 0.9 copy-start.5
  14.5 0.9 copy-start.6
  15.4 0.8 copy-start.7
  19.5 96.2 %all-gather.8.cloned.1.call-start = ((), (), s32[]{:S(2)}) async-start(), calls=%async_computation.5 | async-start | bytes 8192000 | tf_op jit(solution)/shard_map/all_gather | solution.py:342
  20.3 210.9 %reduce-scatter.3.cloned.1.call-start = ((), (), s32[]{:S(2)}) async-start(), calls=%async_computation.2 | async-start | bytes 6553600 | tf_op jit(solution)/shard_map/reduce_scatter | solution.py:353
  101.3 286.8 %reduce-scatter.5.cloned.1.call-start = ((), (), s32[]{:S(2)}) async-start(), calls=%async_computation.3 | async-start | bytes 6553600 | tf_op jit(solution)/shard_map/reduce_scatter | solution.py:380
  119.2 11.4 %collective-permute-start.1 = (f32[512,128]{1,0:T(8,128)S(1)}, f32[512,128]{1,0:T(8,128)S(1)}, u32[]{:S(2)}, u32[]{:S(2)}) collective-permute-start(f32[512,128]{1,0:T(8,128)S(1)} %parent.1), channel_id=1, source_target_pairs={{0,4},{4,8},{8,12},{12,0},{1,5},{5,9},{9,13},{13,1},{2,6},{6,10},{... | collective-permute-start | bytes 786440 | tf_op jit(solution)/shard_map/ppermute | solution.py:308
  120.8 41.1 %collective-permute-start.2 = (f32[512,128]{1,0:T(8,128)S(1)}, f32[512,128]{1,0:T(8,128)S(1)}, u32[]{:S(2)}, u32[]{:S(2)}) collective-permute-start(f32[512,128]{1,0:T(8,128)S(1)} %parent.1), channel_id=1, source_target_pairs={{0,8},{4,12},{8,0},{12,4},{1,9},{5,13},{9,1},{13,5},{2,10},{6,14},... | collective-permute-start | bytes 786440 | tf_op jit(solution)/shard_map/ppermute | solution.py:308
  122.2 52.0 %collective-permute-start.3 = (f32[512,128]{1,0:T(8,128)S(1)}, f32[512,128]{1,0:T(8,128)S(1)}, u32[]{:S(2)}, u32[]{:S(2)}) collective-permute-start(f32[512,128]{1,0:T(8,128)S(1)} %parent.1), channel_id=1, source_target_pairs={{0,12},{4,0},{8,4},{12,8},{1,13},{5,1},{9,5},{13,9},{2,14},{6,2},{... | collective-permute-start | bytes 786440 | tf_op jit(solution)/shard_map/ppermute | solution.py:308
  195.7 0.7 copy-start.3
  231.2 161.1 %collective-permute-start = (f32[128,2560]{1,0:T(8,128)}, f32[128,2560]{1,0:T(8,128)S(1)}, u32[]{:S(2)}, u32[]{:S(2)}) collective-permute-start(f32[128,2560]{1,0:T(8,128)} %reduce-scatter.3.cloned.1.call-done.packed), channel_id=1, source_target_pairs={{0,0},{1,4},{2,8},{3,12},{4,1},{5,5},{6,9},{7,13},{8,2},{9,6},{10,... | collective-permute-start | bytes 3932168 | tf_op jit(solution)/shard_map/ppermute | solution.py:290
  388.1 72.5 %collective-permute-start.8 = (f32[128,2560]{1,0:T(8,128)}, f32[128,2560]{1,0:T(8,128)S(1)}, u32[]{:S(2)}, u32[]{:S(2)}) collective-permute-start(f32[128,2560]{1,0:T(8,128)} %reduce-scatter.5.cloned.1.call-done.packed), channel_id=1, source_target_pairs={{0,0},{1,4},{2,8},{3,12},{4,1},{5,5},{6,9},{7,13},{8,2},{9,6},{10,... | collective-permute-start | bytes 3932168 | tf_op jit(solution)/shard_map/ppermute | solution.py:290
  399.6 51.3 %copy-start.1 = (f32[128,2560]{1,0:T(8,128)S(1)}, f32[128,2560]{1,0:T(8,128)}, u32[]{:S(2)}) copy-start(f32[128,2560]{1,0:T(8,128)} %reduce-scatter.3.cloned.1.call-done.packed) | copy-start | bytes 3932164
  400.3 43.2 %collective-permute-start.4 = (f32[256,128]{1,0:T(8,128)}, f32[256,128]{1,0:T(8,128)}, u32[]{:S(2)}, u32[]{:S(2)}) collective-permute-start(f32[256,128]{1,0:T(8,128)} %get-tuple-element.44), channel_id=1, source_target_pairs={{0,4},{4,8},{8,12},{12,0},{1,5},{5,9},{9,13},{13,1},{2,6},{6,10},{... | collective-permute-start | bytes 393224 | tf_op jit(solution)/shard_map/ppermute | solution.py:298
  400.4 44.5 %collective-permute-start.5 = (f32[256,128]{1,0:T(8,128)}, f32[256,128]{1,0:T(8,128)}, u32[]{:S(2)}, u32[]{:S(2)}) collective-permute-start(f32[256,128]{1,0:T(8,128)} %get-tuple-element.46), channel_id=1, source_target_pairs={{0,8},{4,12},{8,0},{12,4},{1,9},{5,13},{9,1},{13,5},{2,10},{6,14},... | collective-permute-start | bytes 393224 | tf_op jit(solution)/shard_map/ppermute | solution.py:298
  404.3 40.6 %collective-permute-start.6 = (f32[256,128]{1,0:T(8,128)}, f32[256,128]{1,0:T(8,128)}, u32[]{:S(2)}, u32[]{:S(2)}) collective-permute-start(f32[256,128]{1,0:T(8,128)} %get-tuple-element.45), channel_id=1, source_target_pairs={{0,12},{4,0},{8,4},{12,8},{1,13},{5,1},{9,5},{13,9},{2,14},{6,2},{... | collective-permute-start | bytes 393224 | tf_op jit(solution)/shard_map/ppermute | solution.py:298
  446.6 8.1 %collective-permute-start.7 = (f32[128,128]{1,0:T(8,128)S(1)}, f32[128,128]{1,0:T(8,128)S(1)}, u32[]{:S(2)}, u32[]{:S(2)}) collective-permute-start(f32[128,128]{1,0:T(8,128)S(1)} %get-tuple-element.54), channel_id=1, source_target_pairs={{0,0},{1,4},{2,8},{3,12},{4,1},{5,5},{6,9},{7,13},{8,2},{9,6},{10,... | collective-permute-start | bytes 196616 | tf_op jit(solution)/shard_map/ppermute | solution.py:290
  450.8 1.9 copy-start.2
  452.8 7.7 %copy-start.4 = (f32[128,512]{1,0:T(8,128)S(1)}, f32[128,512]{1,0:T(8,128)}, u32[]{:S(2)}) copy-start(f32[128,512]{1,0:T(8,128)} %copy-done.3) | copy-start | bytes 786436
  464.8 7.4 %collective-permute-start.10 = (f32[128,128]{1,0:T(8,128)S(1)}, f32[128,128]{1,0:T(8,128)S(1)}, u32[]{:S(2)}, u32[]{:S(2)}) collective-permute-start(f32[128,128]{1,0:T(8,128)S(1)} %get-tuple-element.49), channel_id=1, source_target_pairs={{0,8},{4,12},{8,0},{12,4},{1,9},{5,13},{9,1},{13,5},{2,10},{6,14},... | collective-permute-start | bytes 196616 | tf_op jit(solution)/shard_map/ppermute | solution.py:298
  467.4 7.0 %collective-permute-start.11 = (f32[128,128]{1,0:T(8,128)S(1)}, f32[128,128]{1,0:T(8,128)S(1)}, u32[]{:S(2)}, u32[]{:S(2)}) collective-permute-start(f32[128,128]{1,0:T(8,128)S(1)} %get-tuple-element.48), channel_id=1, source_target_pairs={{0,12},{4,0},{8,4},{12,8},{1,13},{5,1},{9,5},{13,9},{2,14},{6,2},{... | collective-permute-start | bytes 196616 | tf_op jit(solution)/shard_map/ppermute | solution.py:298
  468.1 6.2 %collective-permute-start.9 = (f32[128,128]{1,0:T(8,128)S(1)}, f32[128,128]{1,0:T(8,128)S(1)}, u32[]{:S(2)}, u32[]{:S(2)}) collective-permute-start(f32[128,128]{1,0:T(8,128)S(1)} %get-tuple-element.47), channel_id=1, source_target_pairs={{0,4},{4,8},{8,12},{12,0},{1,5},{5,9},{9,13},{13,1},{2,6},{6,10},{... | collective-permute-start | bytes 196616 | tf_op jit(solution)/shard_map/ppermute | solution.py:298
Sparse Core Ops, SparseCore 0:
  19.7 46.5 all-gather.5
  67.8 47.8 all-gather.7
  118.0 113.1 reduce-scatter.2
  233.4 154.6 reduce-scatter.4

commit v2 on v1

--- a/solution.py
+++ b/solution.py
@@ -62,69 +62,109 @@
     return jax.ShapeDtypeStruct(shape, dtype)
 
 
-def active_order(pattern_one, pattern_two, position, grid_size, capacity):
-    mine = (jnp.arange(grid_size) == position)[None, :]
-    one = jnp.sum(jnp.where(mine, pattern_one.reshape(-1, grid_size), 0), axis=1)
-    two = jnp.sum(jnp.where(mine, pattern_two.reshape(-1, grid_size), 0), axis=1)
-    key = one + two
-    index = jnp.arange(key.shape[0])
-    ahead = (key[None, :] > key[:, None]) | (
-        (key[None, :] == key[:, None]) & (index[None, :] < index[:, None])
-    )
-    rank = jnp.sum(ahead.astype(jnp.int32), axis=1)
-    slots = jnp.arange(capacity)
-    order = jnp.sum(jnp.where(rank[None, :] == slots[:, None], index[None, :], 0), axis=1)
-    return order.astype(jnp.int32), jnp.sum(one), jnp.sum(two)
-
-
-def pack_kernel(cap_one, cap_two, order, counts, f_one, inv_one, f_par, f_root, inv_two, out_one, out_two):
+def plan_kernel(capacities, place, pattern_one, pattern_two, row_order, col_order, info):
+    blocks = row_order.shape[0]
+    grid_size = pattern_one.shape[0] // blocks
+    largest_one, largest_two = jnp.int32(0), jnp.int32(0)
+    counts_one, counts_two = [], []
+    for p in range(grid_size):
+
+        def count(b, carry):
+            return (
+                carry[0] + pattern_one[b * grid_size + p],
+                carry[1] + pattern_two[b * grid_size + p],
+            )
+
+        one, two = lax.fori_loop(0, blocks, count, (jnp.int32(0), jnp.int32(0)))
+        counts_one.append(one)
+        counts_two.append(two)
+        largest_one = jnp.maximum(largest_one, one)
+        largest_two = jnp.maximum(largest_two, two)
+    choice = jnp.int32(len(capacities) - 1)
+    for i in reversed(range(len(capacities) - 1)):
+        fits = (largest_one <= capacities[i][0]) & (largest_two <= capacities[i][1])
+        choice = jnp.where(fits, i, choice)
+    info[4] = choice
+    for axis, order in enumerate((row_order, col_order)):
+        position = place[axis]
+        own_one, own_two = jnp.int32(0), jnp.int32(0)
+        for p in range(grid_size):
+            own_one = jnp.where(position == p, counts_one[p], own_one)
+            own_two = jnp.where(position == p, counts_two[p], own_two)
+        info[2 * axis] = own_one
+        info[2 * axis + 1] = own_two
+
+        def put(b, carry):
+            one = pattern_one[b * grid_size + position]
+            two = pattern_two[b * grid_size + position]
+            slot = jnp.where(two > 0, carry[0], jnp.where(one > 0, carry[1], carry[2]))
+            order[slot] = b
+            return (carry[0] + two, carry[1] + one - two, carry[2] + 1 - one)
+
+        lax.fori_loop(0, blocks, put, (jnp.int32(0), own_two, own_one))
+
+
+def pack_kernel(cap_one, cap_two, order, info, f_one, inv_one, f_par, f_root, inv_two, out_one, out_two):
     width = inv_one.shape[1]
     for i in range(cap_one):
-        out_one[pl.ds(i * B, B), :] = jnp.where(i < counts[0], f_one[order[i]], 0.0)
+        out_one[pl.ds(i * B, B), :] = jnp.where(i < info[0], f_one[order[i]], 0.0)
     out_one[pl.ds(cap_one * B, width), :] = inv_one[...].T
     for i in range(cap_two):
-        out_two[pl.ds(i * B, B), :] = jnp.where(i < counts[1], f_root[order[i]], 0.0)
+        out_two[pl.ds(i * B, B), :] = jnp.where(i < info[1], f_root[order[i]], 0.0)
     out_two[pl.ds(cap_two * B, width), :] = inv_two[...].T
     out_two[pl.ds(cap_two * B + width, f_par.shape[0]), :] = f_par[...]
 
 
-def joined(ref, start, size):
-    return jnp.concatenate([ref[k, pl.ds(start, size), :] for k in range(ref.shape[0])], 1)
-
-
-def solve_one_kernel(cap, gathered, out):
+def joined(refs, start, size):
+    return jnp.concatenate([ref[pl.ds(start, size), :] for ref in refs], 1)
+
+
+def over_rows(first, last, step, body):
+    whole = (last - first) // step
+
+    def turn(i, carry):
+        body(pl.multiple_of(first * B + i * (step * B), B), step * B)
+        return carry
+
+    lax.fori_loop(0, whole, turn, 0)
+    rest = last - first - whole * step
+    if rest:
+        body((first + whole * step) * B, rest * B)
+
+
+def solve_one_kernel(cap, *refs):
+    gathered, out = refs[:-1], refs[-1]
     width = out.shape[0] // 2
     inverse = split(joined(gathered, cap * B, width))
 
-    def step(i, carry):
-        start = pl.multiple_of(i * 2 * B, 2 * B)
-        rows = split(joined(gathered, start, 2 * B))
+    def body(start, size):
+        rows = split(joined(gathered, start, size))
         high, low = split(three_products(lanes_dot, inverse, rows))
-        out[:width, pl.ds(start, 2 * B)] = high
-        out[width:, pl.ds(start, 2 * B)] = low
-        return carry
-
-    lax.fori_loop(0, cap // 2, step, 0)
-
-
-def parent_kernel(cap_two, gathered, out):
+        out[:width, pl.ds(start, size)] = high
+        out[width:, pl.ds(start, size)] = low
+
+    over_rows(0, cap, 4, body)
+
+
+def parent_kernel(cap_two, *refs):
+    gathered, out = refs[:-1], refs[-1]
     width, share = out.shape
     inverse = split(joined(gathered, cap_two * B, width))
     parent = split(joined(gathered, cap_two * B + width, share))
     out[...] = three_products(lanes_dot, inverse, parent)
 
 
-def solve_two_kernel(
-    cap_one, cap_two, place, gathered_one, gathered_two, parents,
-    out_full, out_root, out_lead, out_diag_one, out_diag_two,
-    weight_high, weight_low,
-):
+def solve_two_kernel(cap_one, cap_two, place, parents, *refs):
     grid_size, width, share = parents.shape
+    gathered_one, gathered_two = refs[:grid_size], refs[grid_size:2 * grid_size]
+    out_full, out_root, out_lead, out_diag_one, out_diag_two, weight_high, weight_low = refs[
+        2 * grid_size:
+    ]
     row, col = place[0], place[1]
     for k in range(grid_size):
         total = jnp.zeros((width, share), jnp.float32)
         for m in range(grid_size):
-            piece = gathered_one[k, pl.ds(cap_one * B + m * share, share), :]
+            piece = gathered_one[k][pl.ds(cap_one * B + m * share, share), :]
             total = total + three_products(plain_dot, split(parents[m]), split(piece))
         high, low = split(total)
         weight_high[:, k * share:(k + 1) * share] = high
@@ -143,38 +183,35 @@
     out_diag_two[...] = three_products(lanes_dot, inv_col, inv_row)
     inverse = split(joined(gathered_two, cap_two * B, width))
 
-    def both(i, carry):
-        start = pl.multiple_of(i * 2 * B, 2 * B)
-        own = three_products(lanes_dot, inverse, split(joined(gathered_two, start, 2 * B)))
+    def both(start, size):
+        own = three_products(lanes_dot, inverse, split(joined(gathered_two, start, size)))
         high, low = split(own)
-        out_root[:width, pl.ds(start, 2 * B)] = high
-        out_root[width:, pl.ds(start, 2 * B)] = low
-        other = three_products(lanes_dot, weight, split(joined(gathered_one, start, 2 * B)))
+        out_root[:width, pl.ds(start, size)] = high
+        out_root[width:, pl.ds(start, size)] = low
+        other = three_products(lanes_dot, weight, split(joined(gathered_one, start, size)))
         high, low = split(own - other)
-        out_full[:width, pl.ds(start, 2 * B)] = high
-        out_full[width:, pl.ds(start, 2 * B)] = low
-        return carry
-
-    def first_only(i, carry):
-        start = pl.multiple_of(i * 2 * B, 2 * B)
-        other = three_products(lanes_dot, weight, split(joined(gathered_one, start, 2 * B)))
+        out_full[:width, pl.ds(start, size)] = high
+        out_full[width:, pl.ds(start, size)] = low
+
+    def first_only(start, size):
+        other = three_products(lanes_dot, weight, split(joined(gathered_one, start, size)))
         high, low = split(-other)
-        out_full[:width, pl.ds(start, 2 * B)] = high
-        out_full[width:, pl.ds(start, 2 * B)] = low
-        return carry
-
-    lax.fori_loop(0, cap_two // 2, both, 0)
-    lax.fori_loop(cap_two // 2, cap_one // 2, first_only, 0)
+        out_full[:width, pl.ds(start, size)] = high
+        out_full[width:, pl.ds(start, size)] = low
+
+    over_rows(0, cap_two, 4, both)
+    over_rows(cap_two, cap_one, 4, first_only)
 
 
 def image_kernel(
-    blocks, cap, chunk, order_in, order_out, counts, solved, cov_a, cov_b, out, high, low, total
+    blocks, cap, chunk, group, order_in, order_out, counts, solved, *refs
 ):
+    covs, (out, high, low, total) = refs[:group], refs[group:]
     step = pl.program_id(0)
     width = out.shape[0]
     total[...] = jnp.zeros_like(total)
 
-    @pl.when(2 * step < counts[1])
+    @pl.when(group * step < counts[1])
     def _():
         for lead in range(0, cap, chunk):
             size = min(chunk, cap - lead)
@@ -182,11 +219,11 @@
             @pl.when(lead < counts[0])
             def _():
                 for j in range(size):
-                    for half, cov in enumerate((cov_a, cov_b)):
+                    for part, cov in enumerate(covs):
                         piece = cov[pl.ds(order_in[lead + j], B, stride=blocks), :]
                         piece_high, piece_low = split(piece)
-                        high[half * B:(half + 1) * B, j * B:(j + 1) * B] = piece_high
-                        low[half * B:(half + 1) * B, j * B:(j + 1) * B] = piece_low
+                        high[part * B:(part + 1) * B, j * B:(j + 1) * B] = piece_high
+                        low[part * B:(part + 1) * B, j * B:(j + 1) * B] = piece_low
                 span = slice(lead * B, (lead + size) * B)
                 both = lanes_dot(solved[:, span], high[:, :size * B])
                 more = lanes_dot(solved[:width, span], low[:, :size * B])
@@ -201,31 +238,31 @@
     rows, blocks = covariance.shape[0], covariance.shape[1]
     flat = covariance.reshape(rows * blocks, B)
     chunk = 4
+    group = 4
 
     def place(which):
         def index_map(i, order_in, order_out, counts):
             last = jnp.maximum(counts[1] - 1, 0)
-            return (order_out[jnp.minimum(2 * i + which, last)], 0)
+            return (order_out[jnp.minimum(group * i + which, last)], 0)
 
         return pl.BlockSpec((B * blocks, B), index_map)
 
     grid_spec = pltpu.PrefetchScalarGridSpec(
         num_scalar_prefetch=3,
-        grid=(cap_out // 2,),
+        grid=(pl.cdiv(cap_out, group),),
         in_specs=[
             pl.BlockSpec(solved.shape, lambda i, *_: (0, 0), pipeline_mode=pl.Buffered(1)),
-            place(0),
-            place(1),
+            *[place(which) for which in range(group)],
         ],
-        out_specs=pl.BlockSpec((width, 2 * B), lambda i, *_: (0, i)),
+        out_specs=pl.BlockSpec((width, group * B), lambda i, *_: (0, i)),
         scratch_shapes=[
-            pltpu.VMEM((2 * B, chunk * B), jnp.bfloat16),
-            pltpu.VMEM((2 * B, chunk * B), jnp.bfloat16),
-            pltpu.VMEM((width, 2 * B), jnp.float32),
+            pltpu.VMEM((group * B, chunk * B), jnp.bfloat16),
+            pltpu.VMEM((group * B, chunk * B), jnp.bfloat16),
+            pltpu.VMEM((width, group * B), jnp.float32),
         ],
     )
     return pl.pallas_call(
-        functools.partial(image_kernel, blocks, cap_in, chunk),
+        functools.partial(image_kernel, blocks, cap_in, chunk, group),
         name=name,
         grid_spec=grid_spec,
         out_shape=shape_of((width, cap_out * B)),
@@ -235,7 +272,7 @@
             bytes_accessed=4 * cap_out * B * blocks * B + 8 * width * cap_out * B,
             transcendentals=0,
         ),
-    )(order_in, order_out, counts, solved, flat, flat)
+    )(order_in, order_out, counts, solved, *[flat] * group)
 
 
 def unpack_kernel(blocks, cap, which, order, counts, packed, out):
@@ -250,7 +287,7 @@
 
 def unpack(packed, order, counts, which, blocks, name):
     share, cap = packed.shape[0], packed.shape[1] // B
-    flat = call(
+    return call(
         functools.partial(unpack_kernel, blocks, cap, which),
         name,
         shape_of((share * blocks, B)),
@@ -258,7 +295,6 @@
         1,
         in_specs=[SMEM, SMEM, VMEM],
     )
-    return flat.reshape(share, blocks, 1, B)
 
 
 def gram_one_kernel(image_rows, solved_one, solved_two, out):
@@ -311,9 +347,26 @@
     return gathered
 
 
+def flip(block, axis, bit, grid_size):
+    return lax.ppermute(block, axis, [(i, i ^ bit) for i in range(grid_size)])
+
+
+def gather_cols(block, grid_size):
+    if grid_size != 4:
+        gathered = lax.all_gather(block, "col")
+        position = lax.axis_index("col")
+        return [
+            lax.dynamic_index_in_dim(gathered, position ^ j, 0, keepdims=False)
+            for j in range(grid_size)
+        ]
+    far = flip(block, "col", 2, grid_size)
+    near = flip(block, "col", 1, grid_size)
+    return [block, near, far, flip(far, "col", 1, grid_size)]
+
+
 def run(
-    cap_one, cap_two, root_covariance, factor_one, inverse_one, pattern_one,
-    factor_parent, factor_root, inverse_two, pattern_two,
+    cap_one, cap_two, row_order, col_order, info, place, root_covariance, factor_one, inverse_one,
+    factor_parent, factor_root, inverse_two,
 ):
     grid_size = lax.axis_size("row")
     row = lax.axis_index("row")
@@ -321,34 +374,30 @@
     share, width = inverse_one.shape
     blocks = root_covariance.shape[3]
     covariance = root_covariance.reshape(-1, blocks, B)
-    row_order, row_one, row_two = active_order(pattern_one, pattern_two, row, grid_size, cap_one)
-    col_order, col_one, col_two = active_order(pattern_one, pattern_two, col, grid_size, cap_one)
-    place = jnp.stack([row, col]).astype(jnp.int32)
-    row_counts = jnp.stack([row_one, row_two])
-    col_counts = jnp.stack([col_one, col_two])
+    row_info, col_info = info, info[2:4]
 
     packed_one, packed_two = call(
         functools.partial(pack_kernel, cap_one, cap_two),
         "pack",
         (shape_of((cap_one * B + width, share)), shape_of((cap_two * B + width + share, share))),
         (
-            row_order, row_counts, factor_one.reshape(blocks, B, share), inverse_one,
+            row_order, row_info, factor_one.reshape(blocks, B, share), inverse_one,
             factor_parent, factor_root.reshape(blocks, B, share), inverse_two,
         ),
         1,
         in_specs=[SMEM, SMEM] + [VMEM] * 5,
     )
-    gathered_one = lax.all_gather(packed_one, "col")
-    gathered_two = lax.all_gather(packed_two, "col")
+    gathered_one = gather_cols(packed_one, grid_size)
+    gathered_two = gather_cols(packed_two, grid_size)
 
     solved_one = call(
         functools.partial(solve_one_kernel, cap_one),
         "solve_one",
         shape_of((2 * width, cap_one * B), jnp.bfloat16),
-        (gathered_one,),
+        gathered_one,
         6 * width * width * cap_one * B,
     )
-    counts = jnp.stack([row_one, col_one])
+    counts = jnp.stack([info[0], info[2]])
     image_one = image(covariance, solved_one, row_order, col_order, counts, cap_one, "image_one")
     image_one = lax.psum_scatter(image_one, "row", scatter_dimension=0, tiled=True)
 
@@ -356,7 +405,7 @@
         functools.partial(parent_kernel, cap_two),
         "parent",
         shape_of((width, share)),
-        (gathered_two,),
+        gathered_two,
         6 * width * width * share,
     )
     parents = gather_rows(parent, grid_size, row)
@@ -370,17 +419,17 @@
             shape_of((share, share)),
             shape_of((share, share)),
         ),
-        (place, gathered_one, gathered_two, parents),
+        (place, parents, *gathered_one, *gathered_two),
         6 * width * width * (cap_one + cap_two) * B,
-        in_specs=[SMEM] + [VMEM] * 3,
+        in_specs=[SMEM] + [VMEM] * (1 + 2 * grid_size),
         scratch=[pltpu.VMEM((width, width), jnp.bfloat16)] * 2,
     )
-    counts = jnp.stack([row_one, col_two])
+    counts = jnp.stack([info[0], info[3]])
     image_two = image(covariance, solved_two, row_order, col_order, counts, cap_two, "image_two")
     image_two = lax.psum_scatter(image_two, "row", scatter_dimension=0, tiled=True)
 
     rows_one = swap_grid(image_one, grid_size)
-    cross_one = unpack(image_one, col_order, col_counts, 0, blocks, "cross_one")
+    cross_one = unpack(image_one, col_order, col_info, 0, blocks, "cross_one")
     gram_one = call(
         gram_one_kernel,
         "gram_one",
@@ -388,15 +437,19 @@
         (rows_one, solved_one, solved_two),
         12 * share * width * cap_one * B,
     )
+    image_two, gram_one, cross_one = lax.optimization_barrier((image_two, gram_one, cross_one))
+    rows_two = swap_grid(image_two, grid_size)
     gram_one = scatter_sum(gram_one, grid_size, row)
     block_one = gram_one[:share] + diag_one
     mixed = swap_grid(gram_one[share:], grid_size)
     own_lead = lax.dynamic_slice_in_dim(lead, col * share, share, 1)
-    mixed_all = lax.all_gather(mixed, "col")
-    parent_out = jnp.concatenate([mixed_all[k] for k in range(grid_size)], 1) - lead
-
-    rows_two = swap_grid(image_two, grid_size)
-    cross_two = unpack(image_two, col_order, col_counts, 1, blocks, "cross_two")
+    parent_out = -lead
+    for j, piece in enumerate(gather_cols(mixed, grid_size)):
+        start = (col ^ j) * share
+        here = lax.dynamic_slice_in_dim(parent_out, start, share, 1)
+        parent_out = lax.dynamic_update_slice_in_dim(parent_out, here + piece, start, 1)
+
+    cross_two = unpack(image_two, col_order, col_info, 1, blocks, "cross_two")
     gram_two = call(
         gram_two_kernel,
         "gram_two",
@@ -408,10 +461,40 @@
     return cross_one, block_one, parent_out, cross_two, block_two
 
 
-def local(*arguments):
-    blocks = arguments[0].shape[3]
-    full = blocks + blocks % 2
-    return run(full, full, *arguments)
+def capacities_of(blocks):
+    parts = ((0.7, 0.55), (0.75, 0.6), (0.8, 0.65), (0.9, 0.7)) if blocks >= 16 else ()
+    return [(round(one * blocks), round(two * blocks)) for one, two in parts] + [(blocks, blocks)]
+
+
+def local(
+    root_covariance, factor_one, inverse_one, pattern_one, factor_parent, factor_root, inverse_two,
+    pattern_two,
+):
+    blocks = root_covariance.shape[3]
+    capacities = capacities_of(blocks)
+    place = jnp.stack([lax.axis_index("row"), lax.axis_index("col")]).astype(jnp.int32)
+    row_order, col_order, info = pl.pallas_call(
+        functools.partial(plan_kernel, capacities),
+        name="plan",
+        out_shape=(
+            shape_of((blocks,), jnp.int32), shape_of((blocks,), jnp.int32), shape_of((5,), jnp.int32)
+        ),
+        in_specs=[SMEM] * 3,
+        out_specs=(SMEM,) * 3,
+    )(place, pattern_one, pattern_two)
+    operands = (
+        row_order, col_order, info, place, root_covariance, factor_one, inverse_one,
+        factor_parent, factor_root, inverse_two,
+    )
+    branches = [functools.partial(run, one, two) for one, two in capacities]
+    if len(branches) == 1:
+        results = branches[0](*operands)
+    else:
+        results = lax.switch(info[4], branches, *operands)
+    cross_one, block_one, parent_out, cross_two, block_two = results
+    cross_one = cross_one.reshape(-1, blocks, 1, B)
+    cross_two = cross_two.reshape(-1, blocks, 1, B)
+    return cross_one, block_one, parent_out, cross_two, block_two
 
 
 def solution(mesh):

time: 485 us -> 405 us (0.84); the launches traced: 482 us -> 406 us
  waiting for transfers between devices: 322 us -> 247 us
  Pallas kernels: 97.7 us -> 70.9 us
  starting transfers between devices: 23.5 us -> 39.7 us
  loops' own time: 0 us -> 16.2 us
  blocking collectives: 5.77 us -> 0 us
    reduce_scatter x1, waiting for transfers between devices: 154 us -> 0.28 us  [run(): lax.psum_scatter(image_two, 'row', scatter_dimension=0, tiled=True)]
    ppermute x3, waiting for transfers between devices: 0.01 us -> 107 us  [swap_grid(): return lax.ppermute(block, ('row', 'col'), pairs)]
    ppermute x0 -> x9, waiting for transfers between devices: none -> 62.2 us  [flip(): return lax.ppermute(block, axis, [(i, i ^ bit) for i in range(grid_size)])]
    all_gather x2 -> x0, waiting for transfers between devices: 57.3 us -> none  [the longest x1 44.3 us: run(): gathered_one = lax.all_gather(packed_one, 'col')]
    ppermute x6, waiting for transfers between devices: 44.8 us -> 28.3 us  [scatter_sum(): lax.ppermute(piece, 'row', [(i, (i + shift) % grid_size) for i in range(g...]
    another operation x0 -> x1, loops' own time: none -> 16.2 us  [local(): results = lax.switch(info[4], branches, *operands)]
    reduce_scatter x1, waiting for transfers between devices: 15.5 us -> 0.02 us  [run(): lax.psum_scatter(image_one, 'row', scatter_dimension=0, tiled=True)]
    pallas_call x2 -> x3, Pallas kernels: 42.6 us -> 27.6 us  [the longest x2 25.2 us: image(): pl.pallas_call(functools.partial(image_kernel, blocks, cap_in, chunk, gro...]
  transfers between devices with their start and end apart: 16 -> 23, of which waited for: 11 -> 15; matrix products, arithmetic and copies ran while one was open for 2% -> 3% of each run, Pallas kernels for 19% -> 11%
where the time goes in v2:
time: 405 us; the launch traced here: 406 us
  waiting for transfers between devices  247 us (61%)
  Pallas kernels  70.9 us (18%)
  starting transfers between devices  39.7 us (10%)
  loops' own time  16.2 us (4%)
  between operations  15.2 us (4%)
  other arithmetic  10.2 us (3%)
  local copies, waits for them, and re-layouts  7.14 us (2%)
    ppermute x3, waiting for transfers between devices, swap_grid(): return lax.ppermute(block, ('row', 'col'), pairs)  107 us
    ppermute x9, waiting for transfers between devices, flip(): return lax.ppermute(block, axis, [(i, i ^ bit) for i in range(grid_size)])  62.2 us
    ppermute x3, waiting for transfers between devices, gather_rows(): lax.ppermute(block, 'row', [(i, (i + shift) % grid_size) for i in range(g...  49.2 us
    pallas_call x8, Pallas kernels, call(): pl.pallas_call(kernel, name=name, out_shape=out_shape, in_specs=in_specs...  43.3 us
    ppermute x6, waiting for transfers between devices, scatter_sum(): lax.ppermute(piece, 'row', [(i, (i + shift) % grid_size) for i in range(g...  28.3 us
    pallas_call x2, Pallas kernels, image(): pl.pallas_call(functools.partial(image_kernel, blocks, cap_in, chunk, gro...  25.2 us
    another operation x1, loops' own time, local(): results = lax.switch(info[4], branches, *operands)  16.2 us
    ppermute x3, starting transfers between devices, gather_rows(): lax.ppermute(block, 'row', [(i, (i + shift) % grid_size) for i in range(g...  13.4 us
  transfers between devices with their start and end apart: 23, of which 15 were waited for; matrix products, arithmetic and copies ran while one was open for 3% of the time, Pallas kernels for 11%

profile of v2, /device:TPU:14, one launch (start us, length us, event | category | flops | bytes accessed | tf_op | source)
XLA Modules:
  0.0 406.4 jit_solution(13325616100276589268)
XLA Ops:
  10.8 387.6 %conditional.1 = (f32[2560,128]{1,0:T(8,128)}, f32[128,128]{1,0:T(8,128)}, f32[128,512]{1,0:T(8,128)}, f32[128,128]{1,0:T(8,128)S(1)}, f32[128,20,1,128]{3,2,1,0:T(1,128)}) conditional(s32[]{:T(128)} %bitcast.92, (s32[5]{0:T(128)S(1)}, f32[20,1,128,128]{3,2,1,0:T(8,128)}, f32[20,1,128,128]{3,2,1,0:T(8,128)}, ...), branch_computations={%region_0.3_spmd, %region_3.6_spmd, %region_6.9_spmd, %region_9.12... | conditional | flops 55566467072 | bytes 312609120 | solution.py:493
  16.3 3.2 pack.7
  20.1 30.2 %collective-permute-done.49.refs_2_ = f32[2560,128]{1,0:T(8,128)S(1)} collective-permute-done((f32[2560,128]{1,0:T(8,128)}, f32[2560,128]{1,0:T(8,128)S(1)}, u32[]{:S(2)}, u32[]{:S(2)}) %collective-permute-start.49) | collective-permute-done | bytes 1310752 | tf_op jit(solution)/shard_map/cond/branch_2_fun/ppermute | solution.py:351
  55.9 8.4 %solve_one.7.solved.solved_one = bf16[1024,2048]{1,0:T(8,128)(2,1)} custom-call(f32[2560,128]{1,0:T(8,128)S(1)} %copy-done.18, f32[2560,128]{1,0:T(8,128)} %copy-done.44, f32[2560,128]{1,0:T(8,128)} %copy-done.43, f32[2560,128]{1,0:T(8,128)} %copy-done.45), custom_call_target="tpu_custom_call" | custom-call | flops 3221225472 | bytes 9437184 | tf_op jit(solution)/shard_map/cond/branch_2_fun/solve_one/pallas_call | solution.py:49
  64.3 13.8 %image_one.7 = f32[512,2048]{1,0:T(8,128)} custom-call(s32[20]{0:T(128)S(1)} %get-tuple-element.141.order.order_in, s32[20]{0:T(128)S(1)} %get-tuple-element.142.order_out.order, s32[2]{0:T(128)S(1)} %pad_add_fusion.5.counts, bf16[1024,2048]{1,0:T(8,128)(2,1)} %solve_one.7.solved.solved_one, f32[51200,128]{1,0:T(8,128)} %bitcast.220, ...), custom_call_target="tpu_custom_call" | custom-call | flops 12884901888 | bytes 29360128 | tf_op jit(solution)/shard_map/cond/branch_2_fun/image_one/pallas_call | solution.py:264
  81.3 25.6 %collective-permute-done.43.refs_2_.refs_6_ = f32[2304,128]{1,0:T(8,128)S(1)} collective-permute-done((f32[2304,128]{1,0:T(8,128)S(1)}, f32[2304,128]{1,0:T(8,128)S(1)}, u32[]{:S(2)}, u32[]{:S(2)}) %collective-permute-start.43) | collective-permute-done | bytes 1179680 | tf_op jit(solution)/shard_map/cond/branch_2_fun/ppermute | solution.py:351
  114.2 5.7 %collective-permute-start.45 = (f32[512,128]{1,0:T(8,128)S(1)}, f32[512,128]{1,0:T(8,128)S(1)}, u32[]{:S(2)}, u32[]{:S(2)}) collective-permute-start(f32[512,128]{1,0:T(8,128)S(1)} %parent.7), channel_id=1, source_target_pairs={{0,4},{4,8},{8,12},{12,0},{1,5},{5,9},{9,13},{13,1},{2,6},{6,10},{... | collective-permute-start | bytes 786440 | tf_op jit(solution)/shard_map/cond/branch_2_fun/ppermute | solution.py:344
  121.3 5.7 %collective-permute-start.46 = (f32[512,128]{1,0:T(8,128)S(1)}, f32[512,128]{1,0:T(8,128)S(1)}, u32[]{:S(2)}, u32[]{:S(2)}) collective-permute-start(f32[512,128]{1,0:T(8,128)S(1)} %parent.7), channel_id=1, source_target_pairs={{0,8},{4,12},{8,0},{12,4},{1,9},{5,13},{9,1},{13,5},{2,10},{6,14},... | collective-permute-start | bytes 786440 | tf_op jit(solution)/shard_map/cond/branch_2_fun/ppermute | solution.py:344
  129.1 10.7 %collective-permute-done.45 = f32[512,128]{1,0:T(8,128)S(1)} collective-permute-done((f32[512,128]{1,0:T(8,128)S(1)}, f32[512,128]{1,0:T(8,128)S(1)}, u32[]{:S(2)}, u32[]{:S(2)}) %collective-permute-start.45) | collective-permute-done | bytes 262176 | tf_op jit(solution)/shard_map/cond/branch_2_fun/ppermute | solution.py:344
  139.7 31.6 %collective-permute-done.46 = f32[512,128]{1,0:T(8,128)S(1)} collective-permute-done((f32[512,128]{1,0:T(8,128)S(1)}, f32[512,128]{1,0:T(8,128)S(1)}, u32[]{:S(2)}, u32[]{:S(2)}) %collective-permute-start.46) | collective-permute-done | bytes 262176 | tf_op jit(solution)/shard_map/cond/branch_2_fun/ppermute | solution.py:344
  171.4 6.9 %collective-permute-done.47 = f32[512,128]{1,0:T(8,128)S(1)} collective-permute-done((f32[512,128]{1,0:T(8,128)S(1)}, f32[512,128]{1,0:T(8,128)S(1)}, u32[]{:S(2)}, u32[]{:S(2)}) %collective-permute-start.47) | collective-permute-done | bytes 262176 | tf_op jit(solution)/shard_map/cond/branch_2_fun/ppermute | solution.py:344
  178.3 16.1 %solve_two.7 = (bf16[1024,2048]{1,0:T(8,128)(2,1)}, bf16[1024,1664]{1,0:T(8,128)(2,1)}, f32[128,512]{1,0:T(8,128)S(1)}, f32[128,128]{1,0:T(8,128)S(1)}, f32[128,128]{1,0:T(8,128)S(1)}) custom-call(s32[2]{0:T(128)S(1)} %copy-done.53, f32[4,512,128]{2,1,0:T(8,128)S(1)} %bitcast_dynamic-update-slice_fusion.8.parents, f32[2560,128]{1,0:T(8,128)} %get-tuple-element.151.refs_0_, ...), custom_call_target="tpu_custom_call" | custom-call | flops 5838471168 | bytes 19005448 | tf_op jit(solution)/shard_map/cond/branch_2_fun/solve_two/pallas_call | solution.py:49
  194.5 11.5 %image_two.7 = f32[512,1664]{1,0:T(8,128)} custom-call(s32[20]{0:T(128)S(1)} %get-tuple-element.141.order.order_in, s32[20]{0:T(128)S(1)} %get-tuple-element.142.order_out.order, s32[2]{0:T(128)S(1)} %pad_add_fusion.4.counts, bf16[1024,2048]{1,0:T(8,128)(2,1)} %get-tuple-element.152.solved.solved_two, f32[51200,128]{1,0:T(8,128)} %bitcast.224, ...), custom_call_target="tpu_custom_call" | custom-call | flops 10468982784 | bytes 23855104 | tf_op jit(solution)/shard_map/cond/branch_2_fun/image_two/pallas_call | solution.py:264
  206.0 3.1 collective-permute-start.51
  212.3 91.8 %collective-permute-done.51.image_rows = f32[128,2048]{1,0:T(8,128)S(1)} collective-permute-done((f32[128,2048]{1,0:T(8,128)}, f32[128,2048]{1,0:T(8,128)S(1)}, u32[]{:S(2)}, u32[]{:S(2)}) %collective-permute-start.51) | collective-permute-done | bytes 1048608 | tf_op jit(solution)/shard_map/cond/branch_2_fun/ppermute | solution.py:326
  304.1 6.1 %gram_one.7 = f32[4,256,128]{2,1,0:T(8,128)S(1)} custom-call(f32[128,2048]{1,0:T(8,128)S(1)} %collective-permute-done.51.image_rows, bf16[1024,2048]{1,0:T(8,128)(2,1)} %solve_one.7.solved.solved_one, bf16[1024,2048]{1,0:T(8,128)(2,1)} %get-tuple-element.152.solved.solved_two), custom_call_target="tpu_custom_call" | custom-call | flops 1610612736 | bytes 9961472 | tf_op jit(solution)/shard_map/cond/branch_2_fun/gram_one/pallas_call | solution.py:49
  313.0 3.8 collective-permute-start.53
  316.8 3.6 collective-permute-start.59
  322.5 21.8 %collective-permute-done.53 = f32[256,128]{1,0:T(8,128)S(1)} collective-permute-done((f32[256,128]{1,0:T(8,128)S(1)}, f32[256,128]{1,0:T(8,128)S(1)}, u32[]{:S(2)}, u32[]{:S(2)}) %collective-permute-start.53) | collective-permute-done | bytes 131104 | tf_op jit(solution)/shard_map/cond/branch_2_fun/ppermute | solution.py:334
  344.9 4.4 %collective-permute-start.55 = (f32[128,128]{1,0:T(8,128)S(1)}, f32[128,128]{1,0:T(8,128)S(1)}, u32[]{:S(2)}, u32[]{:S(2)}) collective-permute-start(f32[128,128]{1,0:T(8,128)S(1)} %get-tuple-element.365), channel_id=1, source_target_pairs={{0,0},{1,4},{2,8},{3,12},{4,1},{5,5},{6,9},{7,13},{8,2},{9,6},{10,... | collective-permute-start | bytes 196616 | tf_op jit(solution)/shard_map/cond/branch_2_fun/ppermute | solution.py:326
  352.0 15.2 %collective-permute-done.55 = f32[128,128]{1,0:T(8,128)S(1)} collective-permute-done((f32[128,128]{1,0:T(8,128)S(1)}, f32[128,128]{1,0:T(8,128)S(1)}, u32[]{:S(2)}, u32[]{:S(2)}) %collective-permute-start.55) | collective-permute-done | bytes 65568 | tf_op jit(solution)/shard_map/cond/branch_2_fun/ppermute | solution.py:326
  368.7 3.0 collective-permute-done.57
  374.7 3.2 gram_two.7
  378.0 3.9 collective-permute-start.61
  (83 shorter events, 45.6 us)
Async XLA Ops:
  16.3 189.7 %reduce-scatter.21.cloned.1.call-start = ((), (), s32[]{:S(2)}) async-start(), calls=%async_computation.15 | async-start | bytes 5242880 | tf_op jit(solution)/shard_map/cond/branch_2_fun/reduce_scatter | solution.py:402
  19.6 90.9 %copy-start.4 = (f32[2304,128]{1,0:T(8,128)}, f32[2304,128]{1,0:T(8,128)S(1)}, u32[]{:S(2)}) copy-start(f32[2304,128]{1,0:T(8,128)S(1)} %get-tuple-element.150.refs_0_.refs_4_) | copy-start | bytes 3538948 | tf_op jit(solution)/shard_map/cond
  19.6 30.7 %collective-permute-start.49 = (f32[2560,128]{1,0:T(8,128)}, f32[2560,128]{1,0:T(8,128)S(1)}, u32[]{:S(2)}, u32[]{:S(2)}) collective-permute-start(f32[2560,128]{1,0:T(8,128)} %get-tuple-element.151.refs_0_), channel_id=1, source_target_pairs={{0,2},{1,3},{2,0},{3,1},{4,6},{5,7},{6,4},{7,5},{8,10},{9,11},{10,... | collective-permute-start | bytes 3932168 | tf_op jit(solution)/shard_map/cond/branch_2_fun/ppermute | solution.py:351
  20.1 32.3 %collective-permute-start.48 = (f32[2560,128]{1,0:T(8,128)}, f32[2560,128]{1,0:T(8,128)S(1)}, u32[]{:S(2)}, u32[]{:S(2)}) collective-permute-start(f32[2560,128]{1,0:T(8,128)} %get-tuple-element.151.refs_0_), channel_id=1, source_target_pairs={{0,1},{1,0},{2,3},{3,2},{4,5},{5,4},{6,7},{7,6},{8,9},{9,8},{10,11... | collective-permute-start | bytes 3932168 | tf_op jit(solution)/shard_map/cond/branch_2_fun/ppermute | solution.py:351
  50.3 3.0 collective-permute-start.50
  78.1 232.4 %reduce-scatter.19.cloned.1.call-start = ((), (), s32[]{:S(2)}) async-start(), calls=%async_computation.14 | async-start | bytes 4259840 | tf_op jit(solution)/shard_map/cond/branch_2_fun/reduce_scatter | solution.py:429
  78.2 28.7 %collective-permute-start.43 = (f32[2304,128]{1,0:T(8,128)S(1)}, f32[2304,128]{1,0:T(8,128)S(1)}, u32[]{:S(2)}, u32[]{:S(2)}) collective-permute-start(f32[2304,128]{1,0:T(8,128)S(1)} %get-tuple-element.150.refs_0_.refs_4_), channel_id=1, source_target_pairs={{0,2},{1,3},{2,0},{3,1},{4,6},{5,7},{6,4},{7,5},{8,10},{9,11},{10,... | collective-permute-start | bytes 3538952 | tf_op jit(solution)/shard_map/cond/branch_2_fun/ppermute | solution.py:351
  81.0 27.0 %collective-permute-start.42 = (f32[2304,128]{1,0:T(8,128)S(1)}, f32[2304,128]{1,0:T(8,128)S(1)}, u32[]{:S(2)}, u32[]{:S(2)}) collective-permute-start(f32[2304,128]{1,0:T(8,128)S(1)} %get-tuple-element.150.refs_0_.refs_4_), channel_id=1, source_target_pairs={{0,1},{1,0},{2,3},{3,2},{4,5},{5,4},{6,7},{7,6},{8,9},{9,8},{10,11... | collective-permute-start | bytes 3538952 | tf_op jit(solution)/shard_map/cond/branch_2_fun/ppermute | solution.py:351
  106.9 3.6 collective-permute-start.44
  114.2 25.6 %collective-permute-start.45 = (f32[512,128]{1,0:T(8,128)S(1)}, f32[512,128]{1,0:T(8,128)S(1)}, u32[]{:S(2)}, u32[]{:S(2)}) collective-permute-start(f32[512,128]{1,0:T(8,128)S(1)} %parent.7), channel_id=1, source_target_pairs={{0,4},{4,8},{8,12},{12,0},{1,5},{5,9},{9,13},{13,1},{2,6},{6,10},{... | collective-permute-start | bytes 786440 | tf_op jit(solution)/shard_map/cond/branch_2_fun/ppermute | solution.py:344
  121.3 50.1 %collective-permute-start.46 = (f32[512,128]{1,0:T(8,128)S(1)}, f32[512,128]{1,0:T(8,128)S(1)}, u32[]{:S(2)}, u32[]{:S(2)}) collective-permute-start(f32[512,128]{1,0:T(8,128)S(1)} %parent.7), channel_id=1, source_target_pairs={{0,8},{4,12},{8,0},{12,4},{1,9},{5,13},{9,1},{13,5},{2,10},{6,14},... | collective-permute-start | bytes 786440 | tf_op jit(solution)/shard_map/cond/branch_2_fun/ppermute | solution.py:344
  127.0 51.3 %collective-permute-start.47 = (f32[512,128]{1,0:T(8,128)S(1)}, f32[512,128]{1,0:T(8,128)S(1)}, u32[]{:S(2)}, u32[]{:S(2)}) collective-permute-start(f32[512,128]{1,0:T(8,128)S(1)} %parent.7), channel_id=1, source_target_pairs={{0,12},{4,0},{8,4},{12,8},{1,13},{5,1},{9,5},{13,9},{2,14},{6,2},{... | collective-permute-start | bytes 786440 | tf_op jit(solution)/shard_map/cond/branch_2_fun/ppermute | solution.py:344
  206.0 98.1 %collective-permute-start.51 = (f32[128,2048]{1,0:T(8,128)}, f32[128,2048]{1,0:T(8,128)S(1)}, u32[]{:S(2)}, u32[]{:S(2)}) collective-permute-start(f32[128,2048]{1,0:T(8,128)} %reduce-scatter.21.cloned.1.call-done.packed), channel_id=1, source_target_pairs={{0,0},{1,4},{2,8},{3,12},{4,1},{5,5},{6,9},{7,13},{8,2},{9,6},{10,... | collective-permute-start | bytes 3145736 | tf_op jit(solution)/shard_map/cond/branch_2_fun/ppermute | solution.py:326
  310.5 12.0 %collective-permute-start.52 = (f32[256,128]{1,0:T(8,128)S(1)}, f32[256,128]{1,0:T(8,128)S(1)}, u32[]{:S(2)}, u32[]{:S(2)}) collective-permute-start(f32[256,128]{1,0:T(8,128)S(1)} %get-tuple-element.359), channel_id=1, source_target_pairs={{0,4},{4,8},{8,12},{12,0},{1,5},{5,9},{9,13},{13,1},{2,6},{6,10},{... | collective-permute-start | bytes 393224 | tf_op jit(solution)/shard_map/cond/branch_2_fun/ppermute | solution.py:334
  313.0 31.3 %collective-permute-start.53 = (f32[256,128]{1,0:T(8,128)S(1)}, f32[256,128]{1,0:T(8,128)S(1)}, u32[]{:S(2)}, u32[]{:S(2)}) collective-permute-start(f32[256,128]{1,0:T(8,128)S(1)} %get-tuple-element.361), channel_id=1, source_target_pairs={{0,8},{4,12},{8,0},{12,4},{1,9},{5,13},{9,1},{13,5},{2,10},{6,14},... | collective-permute-start | bytes 393224 | tf_op jit(solution)/shard_map/cond/branch_2_fun/ppermute | solution.py:334
  316.8 27.5 %collective-permute-start.54 = (f32[256,128]{1,0:T(8,128)S(1)}, f32[256,128]{1,0:T(8,128)S(1)}, u32[]{:S(2)}, u32[]{:S(2)}) collective-permute-start(f32[256,128]{1,0:T(8,128)S(1)} %get-tuple-element.360), channel_id=1, source_target_pairs={{0,12},{4,0},{8,4},{12,8},{1,13},{5,1},{9,5},{13,9},{2,14},{6,2},{... | collective-permute-start | bytes 393224 | tf_op jit(solution)/shard_map/cond/branch_2_fun/ppermute | solution.py:334
  316.8 57.9 %collective-permute-start.59 = (f32[128,1664]{1,0:T(8,128)}, f32[128,1664]{1,0:T(8,128)S(1)}, u32[]{:S(2)}, u32[]{:S(2)}) collective-permute-start(f32[128,1664]{1,0:T(8,128)} %reduce-scatter.19.cloned.1.call-done.packed), channel_id=1, source_target_pairs={{0,0},{1,4},{2,8},{3,12},{4,1},{5,5},{6,9},{7,13},{8,2},{9,6},{10,... | collective-permute-start | bytes 2555912 | tf_op jit(solution)/shard_map/cond/branch_2_fun/ppermute | solution.py:326
  344.9 22.3 %collective-permute-start.55 = (f32[128,128]{1,0:T(8,128)S(1)}, f32[128,128]{1,0:T(8,128)S(1)}, u32[]{:S(2)}, u32[]{:S(2)}) collective-permute-start(f32[128,128]{1,0:T(8,128)S(1)} %get-tuple-element.365), channel_id=1, source_target_pairs={{0,0},{1,4},{2,8},{3,12},{4,1},{5,5},{6,9},{7,13},{8,2},{9,6},{10,... | collective-permute-start | bytes 196616 | tf_op jit(solution)/shard_map/cond/branch_2_fun/ppermute | solution.py:326
  367.2 4.5 %collective-permute-start.56 = (f32[128,128]{1,0:T(8,128)S(1)}, f32[128,128]{1,0:T(8,128)S(1)}, u32[]{:S(2)}, u32[]{:S(2)}) collective-permute-start(f32[128,128]{1,0:T(8,128)S(1)} %collective-permute-done.55), channel_id=1, source_target_pairs={{0,1},{1,0},{2,3},{3,2},{4,5},{5,4},{6,7},{7,6},{8,9},{9,8},{10,11... | collective-permute-start | bytes 196616 | tf_op jit(solution)/shard_map/cond/branch_2_fun/ppermute | solution.py:351
  367.2 4.5 %collective-permute-start.57 = (f32[128,128]{1,0:T(8,128)S(1)}, f32[128,128]{1,0:T(8,128)S(1)}, u32[]{:S(2)}, u32[]{:S(2)}) collective-permute-start(f32[128,128]{1,0:T(8,128)S(1)} %collective-permute-done.55), channel_id=1, source_target_pairs={{0,2},{1,3},{2,0},{3,1},{4,6},{5,7},{6,4},{7,5},{8,10},{9,11},{10,... | collective-permute-start | bytes 196616 | tf_op jit(solution)/shard_map/cond/branch_2_fun/ppermute | solution.py:351
  371.7 10.2 %collective-permute-start.58 = (f32[128,128]{1,0:T(8,128)S(1)}, f32[128,128]{1,0:T(8,128)S(1)}, u32[]{:S(2)}, u32[]{:S(2)}) collective-permute-start(f32[128,128]{1,0:T(8,128)S(1)} %collective-permute-done.57), channel_id=1, source_target_pairs={{0,1},{1,0},{2,3},{3,2},{4,5},{5,4},{6,7},{7,6},{8,9},{9,8},{10,11... | collective-permute-start | bytes 196616 | tf_op jit(solution)/shard_map/cond/branch_2_fun/ppermute | solution.py:351
  377.9 5.5 %collective-permute-start.60 = (f32[128,128]{1,0:T(8,128)S(1)}, f32[128,128]{1,0:T(8,128)S(1)}, u32[]{:S(2)}, u32[]{:S(2)}) collective-permute-start(f32[128,128]{1,0:T(8,128)S(1)} %get-tuple-element.362), channel_id=1, source_target_pairs={{0,4},{4,8},{8,12},{12,0},{1,5},{5,9},{9,13},{13,1},{2,6},{6,10},{... | collective-permute-start | bytes 196616 | tf_op jit(solution)/shard_map/cond/branch_2_fun/ppermute | solution.py:334
  378.0 8.2 %collective-permute-start.61 = (f32[128,128]{1,0:T(8,128)S(1)}, f32[128,128]{1,0:T(8,128)S(1)}, u32[]{:S(2)}, u32[]{:S(2)}) collective-permute-start(f32[128,128]{1,0:T(8,128)S(1)} %get-tuple-element.364), channel_id=1, source_target_pairs={{0,8},{4,12},{8,0},{12,4},{1,9},{5,13},{9,1},{13,5},{2,10},{6,14},... | collective-permute-start | bytes 196616 | tf_op jit(solution)/shard_map/cond/branch_2_fun/ppermute | solution.py:334
  381.9 6.0 %collective-permute-start.62 = (f32[128,128]{1,0:T(8,128)S(1)}, f32[128,128]{1,0:T(8,128)S(1)}, u32[]{:S(2)}, u32[]{:S(2)}) collective-permute-start(f32[128,128]{1,0:T(8,128)S(1)} %get-tuple-element.363), channel_id=1, source_target_pairs={{0,12},{4,0},{8,4},{12,8},{1,13},{5,1},{9,5},{13,9},{2,14},{6,2},{... | collective-permute-start | bytes 196616 | tf_op jit(solution)/shard_map/cond/branch_2_fun/ppermute | solution.py:334
  (12 other events, 107.8 us)
Sparse Core Ops, SparseCore 0:
  78.2 111.1 reduce-scatter.20
  206.1 104.3 reduce-scatter.18

commit v3 on v2

--- a/solution.py
+++ b/solution.py
@@ -9,6 +9,7 @@
 
 B = 128
 VMEM_LIMIT = 52 * 1024 * 1024
+GROUP = 4
 VMEM = pl.BlockSpec(memory_space=pltpu.VMEM)
 SMEM = pl.BlockSpec(memory_space=pltpu.SMEM)
 
@@ -104,15 +105,26 @@
         lax.fori_loop(0, blocks, put, (jnp.int32(0), own_two, own_one))
 
 
-def pack_kernel(cap_one, cap_two, order, info, f_one, inv_one, f_par, f_root, inv_two, out_one, out_two):
-    width = inv_one.shape[1]
-    for i in range(cap_one):
-        out_one[pl.ds(i * B, B), :] = jnp.where(i < info[0], f_one[order[i]], 0.0)
-    out_one[pl.ds(cap_one * B, width), :] = inv_one[...].T
-    for i in range(cap_two):
-        out_two[pl.ds(i * B, B), :] = jnp.where(i < info[1], f_root[order[i]], 0.0)
-    out_two[pl.ds(cap_two * B, width), :] = inv_two[...].T
-    out_two[pl.ds(cap_two * B + width, f_par.shape[0]), :] = f_par[...]
+def pack_one_kernel(cap, order, info, factor, inverse, out, out_bare):
+    for i in range(cap):
+        block = jnp.where(i < info[0], factor[order[i]], 0.0)
+        out[pl.ds(i * B, B), :] = block
+        out_bare[pl.ds(i * B, B), :] = block
+    out[pl.ds(cap * B, inverse.shape[1]), :] = inverse[...].T
+
+
+def pack_two_kernel(cap, order, info, place, factor, inverse, *refs):
+    parents, out = refs[:-1], refs[-1]
+    width = inverse.shape[1]
+    share = parents[0].shape[0]
+    grid_size = len(parents)
+    for i in range(cap):
+        out[pl.ds(i * B, B), :] = jnp.where(i < info[1], factor[order[i]], 0.0)
+    out[pl.ds(cap * B, width), :] = inverse[...].T
+    for shift, parent in enumerate(parents):
+        source = lax.rem(place[0] + grid_size - shift, grid_size)
+        start = pl.multiple_of(source * share, share)
+        out[pl.ds(cap * B + width + start, share), :] = parent[...]
 
 
 def joined(refs, start, size):
@@ -132,41 +144,50 @@
         body((first + whole * step) * B, rest * B)
 
 
-def solve_one_kernel(cap, *refs):
-    gathered, out = refs[:-1], refs[-1]
+def solve_rows(inverse, refs, out, cap):
     width = out.shape[0] // 2
-    inverse = split(joined(gathered, cap * B, width))
 
     def body(start, size):
-        rows = split(joined(gathered, start, size))
+        rows = split(joined(refs, start, size))
         high, low = split(three_products(lanes_dot, inverse, rows))
         out[:width, pl.ds(start, size)] = high
         out[width:, pl.ds(start, size)] = low
 
-    over_rows(0, cap, 4, body)
-
-
-def parent_kernel(cap_two, *refs):
+    over_rows(0, cap, GROUP, body)
+
+
+def solve_one_kernel(cap, *refs):
+    gathered, out, out_inverse = refs[:-2], refs[-2], refs[-1]
+    width = out.shape[0] // 2
+    inverse = split(joined(gathered, cap * B, width))
+    out_inverse[...] = stacked(*inverse)
+    solve_rows(inverse, gathered, out, cap)
+
+
+def solve_far_kernel(cap, inverse, *refs):
     gathered, out = refs[:-1], refs[-1]
-    width, share = out.shape
-    inverse = split(joined(gathered, cap_two * B, width))
-    parent = split(joined(gathered, cap_two * B + width, share))
-    out[...] = three_products(lanes_dot, inverse, parent)
-
-
-def solve_two_kernel(cap_one, cap_two, place, parents, *refs):
-    grid_size, width, share = parents.shape
+    width = out.shape[0] // 2
+    if out.shape[1] > cap * B:
+        out[:, cap * B:] = jnp.zeros((2 * width, out.shape[1] - cap * B), out.dtype)
+    solve_rows((inverse[:width, :], inverse[width:, :]), gathered, out, cap)
+
+
+def solve_two_kernel(cap_one, cap_two, grid_size, place, *refs):
     gathered_one, gathered_two = refs[:grid_size], refs[grid_size:2 * grid_size]
-    out_full, out_root, out_lead, out_diag_one, out_diag_two, weight_high, weight_low = refs[
-        2 * grid_size:
-    ]
+    (
+        out_full, out_root, out_lead, out_diag_one, out_diag_two, out_parent, weight_high, weight_low
+    ) = refs[2 * grid_size:]
+    share, width = out_lead.shape
     row, col = place[0], place[1]
+    inverse = split(joined(gathered_two, cap_two * B, width))
+    parent_start = cap_two * B + width
+    parent = split(joined(gathered_two, parent_start, width))
+    solved_parent = split(three_products(lanes_dot, inverse, parent))
+    row_start = parent_start + pl.multiple_of(row * share, share)
+    out_parent[...] = three_products(lanes_dot, inverse, split(joined(gathered_two, row_start, share)))
     for k in range(grid_size):
-        total = jnp.zeros((width, share), jnp.float32)
-        for m in range(grid_size):
-            piece = gathered_one[k][pl.ds(cap_one * B + m * share, share), :]
-            total = total + three_products(plain_dot, split(parents[m]), split(piece))
-        high, low = split(total)
+        piece = split(gathered_one[k][pl.ds(cap_one * B, width), :])
+        high, low = split(three_products(plain_dot, solved_parent, piece))
         weight_high[:, k * share:(k + 1) * share] = high
         weight_low[:, k * share:(k + 1) * share] = low
     weight = (weight_high[...], weight_low[...])
@@ -181,7 +202,6 @@
     inv_row = split(joined(gathered_two, row_start, share))
     inv_col = split(joined(gathered_two, col_start, share))
     out_diag_two[...] = three_products(lanes_dot, inv_col, inv_row)
-    inverse = split(joined(gathered_two, cap_two * B, width))
 
     def both(start, size):
         own = three_products(lanes_dot, inverse, split(joined(gathered_two, start, size)))
@@ -199,8 +219,8 @@
         out_full[:width, pl.ds(start, size)] = high
         out_full[width:, pl.ds(start, size)] = low
 
-    over_rows(0, cap_two, 4, both)
-    over_rows(cap_two, cap_one, 4, first_only)
+    over_rows(0, cap_two, GROUP, both)
+    over_rows(cap_two, cap_one, GROUP, first_only)
 
 
 def image_kernel(
@@ -237,8 +257,8 @@
     cap_in = solved.shape[1] // B
     rows, blocks = covariance.shape[0], covariance.shape[1]
     flat = covariance.reshape(rows * blocks, B)
-    chunk = 4
-    group = 4
+    chunk = GROUP
+    group = GROUP
 
     def place(which):
         def index_map(i, order_in, order_out, counts):
@@ -275,6 +295,70 @@
     )(order_in, order_out, counts, solved, *[flat] * group)
 
 
+def mirror_kernel(blocks, cap, group, order_in, order_out, counts, solved, *refs):
+    covs, (out, high, low) = refs[:group], refs[group:]
+    step = pl.program_id(0)
+    width = out.shape[0]
+
+    @pl.when(step == 0)
+    def _():
+        out[...] = jnp.zeros_like(out)
+
+    @pl.when(group * step < counts[0])
+    def _():
+        for lead in range(0, cap, group):
+            size = min(group, cap - lead)
+
+            @pl.when(lead < counts[1])
+            def _():
+                for j in range(size):
+                    for part, cov in enumerate(covs):
+                        piece = cov[pl.ds(order_out[lead + j], B, stride=blocks), :]
+                        piece_high, piece_low = split(piece)
+                        high[part * B:(part + 1) * B, j * B:(j + 1) * B] = piece_high
+                        low[part * B:(part + 1) * B, j * B:(j + 1) * B] = piece_low
+                both = plain_dot(solved[...], high[:, :size * B])
+                more = plain_dot(solved[:width, :], low[:, :size * B])
+                out[:, lead * B:(lead + size) * B] += both[:width] + both[width:] + more
+
+
+def mirror_image(covariance, solved, order_in, order_out, counts, cap, name):
+    width = solved.shape[0] // 2
+    rows, blocks = covariance.shape[0], covariance.shape[1]
+    flat = covariance.reshape(rows * blocks, B)
+    group = GROUP
+
+    def place(which):
+        def index_map(i, order_in, order_out, counts):
+            last = jnp.maximum(counts[0] - 1, 0)
+            return (order_in[jnp.minimum(group * i + which, last)], 0)
+
+        return pl.BlockSpec((B * blocks, B), index_map)
+
+    grid_spec = pltpu.PrefetchScalarGridSpec(
+        num_scalar_prefetch=3,
+        grid=(solved.shape[1] // (group * B),),
+        in_specs=[
+            pl.BlockSpec((2 * width, group * B), lambda i, *_: (0, i)),
+            *[place(which) for which in range(group)],
+        ],
+        out_specs=pl.BlockSpec((width, cap * B), lambda i, *_: (0, 0)),
+        scratch_shapes=[pltpu.VMEM((group * B, group * B), jnp.bfloat16)] * 2,
+    )
+    return pl.pallas_call(
+        functools.partial(mirror_kernel, blocks, cap, group),
+        name=name,
+        grid_spec=grid_spec,
+        out_shape=shape_of((width, cap * B)),
+        compiler_params=pltpu.CompilerParams(vmem_limit_bytes=VMEM_LIMIT),
+        cost_estimate=pl.CostEstimate(
+            flops=6 * width * cap * B * cap * B,
+            bytes_accessed=4 * cap * B * blocks * B + 8 * width * cap * B,
+            transcendentals=0,
+        ),
+    )(order_in, order_out, counts, solved, *[flat] * group)
+
+
 def unpack_kernel(blocks, cap, which, order, counts, packed, out):
     share = packed.shape[0]
     out[...] = jnp.zeros_like(out)
@@ -337,14 +421,25 @@
     return total
 
 
-def gather_rows(block, grid_size, position):
-    gathered = jnp.zeros((grid_size,) + block.shape, block.dtype)
-    gathered = lax.dynamic_update_index_in_dim(gathered, block, position, 0)
-    for shift in range(1, grid_size):
-        other = lax.ppermute(block, "row", [(i, (i + shift) % grid_size) for i in range(grid_size)])
-        source = lax.rem(position + grid_size - shift, grid_size)
-        gathered = lax.dynamic_update_index_in_dim(gathered, other, source, 0)
-    return gathered
+def gather_rows(block, grid_size):
+    return [block] + [
+        lax.ppermute(block, "row", [(i, (i + shift) % grid_size) for i in range(grid_size)])
+        for shift in range(1, grid_size)
+    ]
+
+
+def plane_sum(partial, grid_size, col):
+    if grid_size != 4:
+        return lax.psum_scatter(partial, "col", scatter_dimension=0, tiled=True)
+    share = partial.shape[0] // grid_size
+    core, chip = col % 2, col // 2
+    pieces = partial.reshape(2, 2, share, partial.shape[1])
+    away = lax.dynamic_index_in_dim(pieces, 1 - core, 1, keepdims=False)
+    stay = lax.dynamic_index_in_dim(pieces, core, 1, keepdims=False)
+    pieces = stay + flip(away, "col", 1, grid_size)
+    away = lax.dynamic_index_in_dim(pieces, 1 - chip, 0, keepdims=False)
+    stay = lax.dynamic_index_in_dim(pieces, chip, 0, keepdims=False)
+    return stay + flip(away, "col", 2, grid_size)
 
 
 def flip(block, axis, bit, grid_size):
@@ -374,43 +469,43 @@
     share, width = inverse_one.shape
     blocks = root_covariance.shape[3]
     covariance = root_covariance.reshape(-1, blocks, B)
-    row_info, col_info = info, info[2:4]
-
-    packed_one, packed_two = call(
-        functools.partial(pack_kernel, cap_one, cap_two),
-        "pack",
-        (shape_of((cap_one * B + width, share)), shape_of((cap_two * B + width + share, share))),
+    col_info = info[2:4]
+
+    packed_one, bare_one = call(
+        functools.partial(pack_one_kernel, cap_one),
+        "pack_one",
+        (shape_of((cap_one * B + width, share)), shape_of((cap_one * B, share))),
+        (row_order, info, factor_one.reshape(blocks, B, share), inverse_one),
+        1,
+        in_specs=[SMEM, SMEM, VMEM, VMEM],
+    )
+    all_rows = lax.all_gather(bare_one, "row")
+    gathered_one = gather_cols(packed_one, grid_size)
+    packed_two = call(
+        functools.partial(pack_two_kernel, cap_two),
+        "pack_two",
+        shape_of((cap_two * B + 2 * width, share)),
         (
-            row_order, row_info, factor_one.reshape(blocks, B, share), inverse_one,
-            factor_parent, factor_root.reshape(blocks, B, share), inverse_two,
+            row_order, info, place, factor_root.reshape(blocks, B, share), inverse_two,
+            *gather_rows(factor_parent, grid_size),
         ),
         1,
-        in_specs=[SMEM, SMEM] + [VMEM] * 5,
-    )
-    gathered_one = gather_cols(packed_one, grid_size)
+        in_specs=[SMEM] * 3 + [VMEM] * (2 + grid_size),
+    )
     gathered_two = gather_cols(packed_two, grid_size)
 
-    solved_one = call(
+    solved_one, lead_inverse = call(
         functools.partial(solve_one_kernel, cap_one),
         "solve_one",
-        shape_of((2 * width, cap_one * B), jnp.bfloat16),
+        (
+            shape_of((2 * width, cap_one * B), jnp.bfloat16),
+            shape_of((2 * width, width), jnp.bfloat16),
+        ),
         gathered_one,
         6 * width * width * cap_one * B,
     )
-    counts = jnp.stack([info[0], info[2]])
-    image_one = image(covariance, solved_one, row_order, col_order, counts, cap_one, "image_one")
-    image_one = lax.psum_scatter(image_one, "row", scatter_dimension=0, tiled=True)
-
-    parent = call(
-        functools.partial(parent_kernel, cap_two),
-        "parent",
-        shape_of((width, share)),
-        gathered_two,
-        6 * width * width * share,
-    )
-    parents = gather_rows(parent, grid_size, row)
-    solved_two, solved_root, lead, diag_one, diag_two = call(
-        functools.partial(solve_two_kernel, cap_one, cap_two),
+    solved_two, solved_root, lead, diag_one, diag_two, parent = call(
+        functools.partial(solve_two_kernel, cap_one, cap_two, grid_size),
         "solve_two",
         (
             shape_of((2 * width, cap_one * B), jnp.bfloat16),
@@ -418,17 +513,34 @@
             shape_of((share, width)),
             shape_of((share, share)),
             shape_of((share, share)),
-        ),
-        (place, parents, *gathered_one, *gathered_two),
+            shape_of((width, share)),
+        ),
+        (place, *gathered_one, *gathered_two),
         6 * width * width * (cap_one + cap_two) * B,
-        in_specs=[SMEM] + [VMEM] * (1 + 2 * grid_size),
+        in_specs=[SMEM] + [VMEM] * (2 * grid_size),
         scratch=[pltpu.VMEM((width, width), jnp.bfloat16)] * 2,
     )
     counts = jnp.stack([info[0], info[3]])
     image_two = image(covariance, solved_two, row_order, col_order, counts, cap_two, "image_two")
     image_two = lax.psum_scatter(image_two, "row", scatter_dimension=0, tiled=True)
 
-    rows_one = swap_grid(image_one, grid_size)
+    far_rows = []
+    for j in range(grid_size):
+        piece = lax.dynamic_index_in_dim(all_rows, col ^ j, 0, keepdims=False)
+        far_rows.append(flip(piece, "col", j, grid_size) if j else piece)
+    solved_far = call(
+        functools.partial(solve_far_kernel, cap_one),
+        "solve_far",
+        shape_of((2 * width, pl.cdiv(cap_one, GROUP) * GROUP * B), jnp.bfloat16),
+        (lead_inverse, *far_rows),
+        6 * width * width * cap_one * B,
+    )
+    counts = jnp.stack([info[2], info[0]])
+    rows_one = mirror_image(
+        covariance, solved_far, col_order, row_order, counts, cap_one, "image_one"
+    )
+    rows_one = plane_sum(rows_one, grid_size, col)
+    image_one = swap_grid(rows_one, grid_size)
     cross_one = unpack(image_one, col_order, col_info, 0, blocks, "cross_one")
     gram_one = call(
         gram_one_kernel,
@@ -437,7 +549,6 @@
         (rows_one, solved_one, solved_two),
         12 * share * width * cap_one * B,
     )
-    image_two, gram_one, cross_one = lax.optimization_barrier((image_two, gram_one, cross_one))
     rows_two = swap_grid(image_two, grid_size)
     gram_one = scatter_sum(gram_one, grid_size, row)
     block_one = gram_one[:share] + diag_one

time: 405 us -> 346 us (0.85)
  waiting for transfers between devices: 247 us -> 169 us
  Pallas kernels: 70.9 us -> 97.8 us
  starting transfers between devices: 39.7 us -> 28.1 us
  other arithmetic: 10.2 us -> 15.4 us
  loops' own time: 16.2 us -> 11.3 us
    ppermute x3, waiting for transfers between devices: 107 us -> 18.6 us  [swap_grid(): return lax.ppermute(block, ('row', 'col'), pairs)]
    ppermute x3, waiting for transfers between devices: 49.2 us -> 3.15 us  [gather_rows(): lax.ppermute(block, 'row', [(i, (i + shift) % grid_size) for i in range(g...]
    ppermute x9 -> x14, waiting for transfers between devices: 62.2 us -> 95.8 us  [flip(): return lax.ppermute(block, axis, [(i, i ^ bit) for i in range(grid_size)])]
    pallas_call x0 -> x1, Pallas kernels: none -> 24.4 us  [mirror_image(): pl.pallas_call(functools.partial(mirror_kernel, blocks, cap, group), name...]
    ppermute x6, waiting for transfers between devices: 28.3 us -> 51.1 us  [scatter_sum(): lax.ppermute(piece, 'row', [(i, (i + shift) % grid_size) for i in range(g...]
    ppermute x3, starting transfers between devices: 13.4 us -> 5.57 us  [gather_rows(): lax.ppermute(block, 'row', [(i, (i + shift) % grid_size) for i in range(g...]
    pallas_call x8 -> x9, Pallas kernels: 43.3 us -> 51.1 us  [call(): pl.pallas_call(kernel, name=name, out_shape=out_shape, in_specs=in_specs...]
    squeeze x0 -> x3, local copies, waits for them, and re-layouts: none -> 5.59 us  [the longest x1 3.81 us: run(): piece = lax.dynamic_index_in_dim(all_rows, col ^ j, 0, keepdims=False)]
  transfers between devices with their start and end apart: 23 -> 28, of which waited for: 15 -> 12; matrix products, arithmetic and copies ran while one was open for 3% -> 5% of each run, Pallas kernels for 11% -> 26%
where the time goes in v3:
time: 346 us
  waiting for transfers between devices  169 us (49%)
  Pallas kernels  97.8 us (28%)
  starting transfers between devices  28.1 us (8%)
  other arithmetic  15.4 us (4%)
  between operations  15 us (4%)
  loops' own time  11.3 us (3%)
  local copies, waits for them, and re-layouts  9.34 us (3%)
    ppermute x14, waiting for transfers between devices, flip(): return lax.ppermute(block, axis, [(i, i ^ bit) for i in range(grid_size)])  95.8 us
    pallas_call x9, Pallas kernels, call(): pl.pallas_call(kernel, name=name, out_shape=out_shape, in_specs=in_specs...  51.1 us
    ppermute x6, waiting for transfers between devices, scatter_sum(): lax.ppermute(piece, 'row', [(i, (i + shift) % grid_size) for i in range(g...  51.1 us
    pallas_call x1, Pallas kernels, mirror_image(): pl.pallas_call(functools.partial(mirror_kernel, blocks, cap, group), name...  24.4 us
    pallas_call x1, Pallas kernels, image(): pl.pallas_call(functools.partial(image_kernel, blocks, cap_in, chunk, gro...  19.9 us
    ppermute x3, waiting for transfers between devices, swap_grid(): return lax.ppermute(block, ('row', 'col'), pairs)  18.6 us
    another operation x1, loops' own time, local(): results = lax.switch(info[4], branches, *operands)  11.3 us
    ppermute x6, starting transfers between devices, scatter_sum(): lax.ppermute(piece, 'row', [(i, (i + shift) % grid_size) for i in range(g...  9.05 us
  transfers between devices with their start and end apart: 28, of which 12 were waited for; matrix products, arithmetic and copies ran while one was open for 5% of the time, Pallas kernels for 26%

profile of v3, /device:TPU:14, one launch (start us, length us, event | category | flops | bytes accessed | tf_op | source)
XLA Modules:
  0.0 345.5 jit_solution(13159084848810683343)
XLA Ops:
  10.8 327.5 %conditional.1 = (f32[128,128]{1,0:T(8,128)}, f32[128,512]{1,0:T(8,128)}, f32[128,128]{1,0:T(8,128)}, f32[128,20,1,128]{3,2,1,0:T(1,128)}, f32[128,20,1,128]{3,2,1,0:T(1,128)}) conditional(s32[]{:T(128)} %bitcast.127, (s32[5]{0:T(128)S(1)}, f32[20,1,128,128]{3,2,1,0:T(8,128)}, s32[20]{0:T(128)S(1)}, ...), branch_computations={%region_0.2_spmd, %region_2.4_spmd, %region_4.6_spmd, %region_6.8_... | conditional | flops 59392655360 | bytes 353635424 | solution.py:604
  14.6 3.0 pack_one.6
  18.2 2.6 collective-permute-start.35
  20.8 2.5 collective-permute-start.34
  30.2 29.8 %collective-permute-done.38.refs_6_ = f32[2560,128]{1,0:T(8,128)} collective-permute-done((f32[2560,128]{1,0:T(8,128)S(1)}, f32[2560,128]{1,0:T(8,128)}, u32[]{:S(2)}, u32[]{:S(2)}) %collective-permute-start.38) | collective-permute-done | bytes 1310752 | tf_op jit(solution)/shard_map/cond/branch_1_fun/ppermute | solution.py:446
  60.5 24.3 %collective-permute-done.27.refs_2_ = f32[2432,128]{1,0:T(8,128)} collective-permute-done((f32[2432,128]{1,0:T(8,128)S(1)}, f32[2432,128]{1,0:T(8,128)}, u32[]{:S(2)}, u32[]{:S(2)}) %collective-permute-start.27) | collective-permute-done | bytes 1245216 | tf_op jit(solution)/shard_map/cond/branch_1_fun/ppermute | solution.py:446
  88.1 17.2 %solve_two.6 = (bf16[1024,1920]{1,0:T(8,128)(2,1)}, bf16[1024,1536]{1,0:T(8,128)(2,1)}, f32[128,512]{1,0:T(8,128)S(1)}, f32[128,128]{1,0:T(8,128)S(1)}, f32[128,128]{1,0:T(8,128)S(1)}, /*index=5*/f32[512,128]{1,0:T(8,128)S(1)}) custom-call(s32[2]{0:T(128)S(1)} %get-tuple-element.132.place, f32[2432,128]{1,0:T(8,128)S(1)} %copy-done.26, ...), custom_call_target="tpu_custom_call" | custom-call | flops 5435817984 | bytes 17956872 | tf_op jit(solution)/shard_map/cond/branch_1_fun/solve_two/pallas_call | solution.py:50
  106.1 3.8 %dynamic-slice_bitcast_fusion.14 = (f32[1920,128]{1,0:T(8,128)}, f32[1920,128]{1,0:T(8,128)}, f32[1920,128]{1,0:T(8,128)}, f32[1920,128]{1,0:T(8,128)S(1)}) fusion(f32[4,1920,128]{2,1,0:T(8,128)} %bitcast.321, s32[]{:T(128)S(6)} %select_n.272, s32[]{:T(128)S(6)} %select_n.271, s32[]{:T(128)S(6)} %select_n.270, s32[]{:T(128)S(6)} %select_n.269), kind=kLoop, calls=%fused_computation.33 | loop fusion | bytes 7864336 | tf_op jit(solution)/shard_map/cond/branch_1_fun/jit(dynamic_index_in_dim)/squeeze | solution.py:529
  112.0 19.9 %image_two.6 = f32[512,1536]{1,0:T(8,128)} custom-call(s32[20]{0:T(128)S(1)} %get-tuple-element.123.order.order_out.order_in, s32[20]{0:T(128)S(1)} %get-tuple-element.122.order_in.order_out.order, s32[2]{0:T(128)S(1)} %pad_add_fusion.3.counts, bf16[1024,1920]{1,0:T(8,128)(2,1)} %get-tuple-element.136.solved_two.solved, f32[51200,128]{1,0:T(8,128)} %bitcast.266, ...), custom_call_target="tpu_custom_call" | custom-call | flops 9059696640 | bytes 22020096 | tf_op jit(solution)/shard_map/cond/branch_1_fun/image_two/pallas_call | solution.py:284
  132.0 8.6 %solve_one.6 = (bf16[1024,1920]{1,0:T(8,128)(2,1)}, bf16[1024,512]{1,0:T(8,128)(2,1)S(1)}) custom-call(f32[2432,128]{1,0:T(8,128)} %get-tuple-element.127.refs_0_, f32[2432,128]{1,0:T(8,128)} %collective-permute-done.26.refs_1_, f32[2432,128]{1,0:T(8,128)} %collective-permute-done.27.refs_2_, f32[2432,128]{1,0:T(8,128)} %collective-permute-done.28.refs_3_), custom_call_target="tpu_custom_call" | custom-call | flops 3019898880 | bytes 9961472 | tf_op jit(solution)/shard_map/cond/branch_1_fun/solve_one/pallas_call | solution.py:50
  141.6 13.8 %collective-permute-done.30.refs_2_ = f32[1920,128]{1,0:T(8,128)} collective-permute-done((f32[1920,128]{1,0:T(8,128)}, f32[1920,128]{1,0:T(8,128)}, u32[]{:S(2)}, u32[]{:S(2)}) %collective-permute-start.30) | collective-permute-done | bytes 983072 | tf_op jit(solution)/shard_map/cond/branch_1_fun/ppermute | solution.py:446
  155.4 8.1 %solve_far.6.solved = bf16[1024,2048]{1,0:T(8,128)(2,1)} custom-call(bf16[1024,512]{1,0:T(8,128)(2,1)} %copy-done.30, f32[1920,128]{1,0:T(8,128)S(1)} %get-tuple-element.355.refs_0_, f32[1920,128]{1,0:T(8,128)S(1)} %collective-permute-done.29.refs_1_, f32[1920,128]{1,0:T(8,128)} %collective-permute-done.30.refs_2_, f32[1920,128]{1,0:T(8,128)} %collective-permute-done.31.refs_3_), custom_call_target="tpu_custom_call" | custom-call | flops 3019898880 | bytes 9175040 | tf_op jit(solution)/shard_map/cond/branch_1_fun/solve_far/pallas_call | solution.py:50
  163.4 24.4 %image_one.6 = f32[512,1920]{1,0:T(8,128)} custom-call(s32[20]{0:T(128)S(1)} %get-tuple-element.122.order_in.order_out.order, s32[20]{0:T(128)S(1)} %get-tuple-element.123.order.order_out.order_in, s32[2]{0:T(128)S(1)} %pad_add_fusion.2.counts, bf16[1024,2048]{1,0:T(8,128)(2,1)} %solve_far.6.solved, f32[51200,128]{1,0:T(8,128)} %bitcast.270, ...), custom_call_target="tpu_custom_call" | custom-call | flops 11324620800 | bytes 27525120 | tf_op jit(solution)/shard_map/cond/branch_1_fun/image_one/pallas_call | solution.py:348
  189.7 4.1 %collective-permute-done.32 = f32[2,128,1920]{2,1,0:T(8,128)} collective-permute-done((f32[2,128,1920]{2,1,0:T(8,128)S(1)}, f32[2,128,1920]{2,1,0:T(8,128)}, u32[]{:S(2)}, u32[]{:S(2)}) %collective-permute-start.32) | collective-permute-done | bytes 1966112 | tf_op jit(solution)/shard_map/cond/branch_1_fun/ppermute | solution.py:446
  196.2 23.9 %collective-permute-done.33 = f32[128,1920]{1,0:T(8,128)} collective-permute-done((f32[128,1920]{1,0:T(8,128)S(1)}, f32[128,1920]{1,0:T(8,128)}, u32[]{:S(2)}, u32[]{:S(2)}) %collective-permute-start.33) | collective-permute-done | bytes 983072 | tf_op jit(solution)/shard_map/cond/branch_1_fun/ppermute | solution.py:446
  221.4 5.8 %gram_one.6 = f32[4,256,128]{2,1,0:T(8,128)S(1)} custom-call(f32[128,1920]{1,0:T(8,128)S(1)} %bitcast_add_fusion.5.image_rows, bf16[1024,1920]{1,0:T(8,128)(2,1)} %get-tuple-element.131.solved_one, bf16[1024,1920]{1,0:T(8,128)(2,1)} %get-tuple-element.136.solved_two.solved), custom_call_target="tpu_custom_call" | custom-call | flops 1509949440 | bytes 9371648 | tf_op jit(solution)/shard_map/cond/branch_1_fun/gram_one/pallas_call | solution.py:50
  228.0 2.5 collective-permute-start.40
  234.0 33.6 %collective-permute-done.40 = f32[256,128]{1,0:T(8,128)} collective-permute-done((f32[256,128]{1,0:T(8,128)}, f32[256,128]{1,0:T(8,128)}, u32[]{:S(2)}, u32[]{:S(2)}) %collective-permute-start.40) | collective-permute-done | bytes 131104 | tf_op jit(solution)/shard_map/cond/branch_1_fun/ppermute | solution.py:418
  267.6 2.8 collective-permute-done.41
  276.7 4.5 %collective-permute-start.51 = (f32[128,1920]{1,0:T(8,128)S(1)}, f32[128,1920]{1,0:T(8,128)S(1)}, u32[]{:S(2)}, u32[]{:S(2)}) collective-permute-start(f32[128,1920]{1,0:T(8,128)S(1)} %bitcast_add_fusion.5.image_rows), channel_id=1, source_target_pairs={{0,0},{1,4},{2,8},{3,12},{4,1},{5,5},{6,9},{7,13},{8,2},{9,6},{10,... | collective-permute-start | bytes 2949128 | tf_op jit(solution)/shard_map/cond/branch_1_fun/ppermute | solution.py:410
  281.3 18.6 %collective-permute-done.43 = f32[128,128]{1,0:T(8,128)S(1)} collective-permute-done((f32[128,128]{1,0:T(8,128)S(1)}, f32[128,128]{1,0:T(8,128)S(1)}, u32[]{:S(2)}, u32[]{:S(2)}) %collective-permute-start.43) | collective-permute-done | bytes 65568 | tf_op jit(solution)/shard_map/cond/branch_1_fun/ppermute | solution.py:410
  301.3 3.1 gram_two.6
  304.4 3.5 %collective-permute-start.48 = (f32[128,128]{1,0:T(8,128)S(1)}, f32[128,128]{1,0:T(8,128)S(1)}, u32[]{:S(2)}, u32[]{:S(2)}) collective-permute-start(f32[128,128]{1,0:T(8,128)S(1)} %get-tuple-element.359), channel_id=1, source_target_pairs={{0,4},{4,8},{8,12},{12,0},{1,5},{5,9},{9,13},{13,1},{2,6},{6,10},{... | collective-permute-start | bytes 196616 | tf_op jit(solution)/shard_map/cond/branch_1_fun/ppermute | solution.py:418
  311.0 13.9 %collective-permute-done.48 = f32[128,128]{1,0:T(8,128)S(1)} collective-permute-done((f32[128,128]{1,0:T(8,128)S(1)}, f32[128,128]{1,0:T(8,128)S(1)}, u32[]{:S(2)}, u32[]{:S(2)}) %collective-permute-start.48) | collective-permute-done | bytes 65568 | tf_op jit(solution)/shard_map/cond/branch_1_fun/ppermute | solution.py:418
  (84 shorter events, 45.0 us)
Async XLA Ops:
  14.6 91.5 %all-gather.13.cloned.1.call-start = ((), (), s32[]{:S(2)}) async-start(), calls=%async_computation.8 | async-start | bytes 4915200 | tf_op jit(solution)/shard_map/cond/branch_1_fun/all_gather | solution.py:482
  17.6 214.3 %reduce-scatter.8.cloned.1.call-start = ((), (), s32[]{:S(2)}) async-start(), calls=%async_computation.7 | async-start | bytes 3932160 | tf_op jit(solution)/shard_map/cond/branch_1_fun/reduce_scatter | solution.py:525
  18.2 7.0 %collective-permute-start.35 = (f32[128,128]{1,0:T(8,128)S(1)}, f32[128,128]{1,0:T(8,128)S(1)}, u32[]{:S(2)}, u32[]{:S(2)}) collective-permute-start(f32[128,128]{1,0:T(8,128)S(1)} %copy-done.41), channel_id=1, source_target_pairs={{0,8},{4,12},{8,0},{12,4},{1,9},{5,13},{9,1},{13,5},{2,10},{6,14},... | collective-permute-start | bytes 196616 | tf_op jit(solution)/shard_map/cond/branch_1_fun/ppermute | solution.py:426
  28.1 31.9 %collective-permute-start.38 = (f32[2560,128]{1,0:T(8,128)S(1)}, f32[2560,128]{1,0:T(8,128)}, u32[]{:S(2)}, u32[]{:S(2)}) collective-permute-start(f32[2560,128]{1,0:T(8,128)S(1)} %pack_two.6.refs_4_), channel_id=1, source_target_pairs={{0,2},{1,3},{2,0},{3,1},{4,6},{5,7},{6,4},{7,5},{8,10},{9,11},{10,... | collective-permute-start | bytes 3932168 | tf_op jit(solution)/shard_map/cond/branch_1_fun/ppermute | solution.py:446
  28.7 56.0 %collective-permute-start.27 = (f32[2432,128]{1,0:T(8,128)S(1)}, f32[2432,128]{1,0:T(8,128)}, u32[]{:S(2)}, u32[]{:S(2)}) collective-permute-start(f32[2432,128]{1,0:T(8,128)S(1)} %copy-done.26), channel_id=1, source_target_pairs={{0,2},{1,3},{2,0},{3,1},{4,6},{5,7},{6,4},{7,5},{8,10},{9,11},{10,... | collective-permute-start | bytes 3735560 | tf_op jit(solution)/shard_map/cond/branch_1_fun/ppermute | solution.py:446
  30.2 57.9 %collective-permute-start.37 = (f32[2560,128]{1,0:T(8,128)S(1)}, f32[2560,128]{1,0:T(8,128)}, u32[]{:S(2)}, u32[]{:S(2)}) collective-permute-start(f32[2560,128]{1,0:T(8,128)S(1)} %pack_two.6.refs_4_), channel_id=1, source_target_pairs={{0,1},{1,0},{2,3},{3,2},{4,5},{5,4},{6,7},{7,6},{8,9},{9,8},{10,11... | collective-permute-start | bytes 3932168 | tf_op jit(solution)/shard_map/cond/branch_1_fun/ppermute | solution.py:446
  60.0 28.1 %collective-permute-start.39 = (f32[2560,128]{1,0:T(8,128)}, f32[2560,128]{1,0:T(8,128)}, u32[]{:S(2)}, u32[]{:S(2)}) collective-permute-start(f32[2560,128]{1,0:T(8,128)} %collective-permute-done.38.refs_6_), channel_id=1, source_target_pairs={{0,1},{1,0},{2,3},{3,2},{4,5},{5,4},{6,7},{7,6},{8,9},{9,8},{10,11... | collective-permute-start | bytes 3932168 | tf_op jit(solution)/shard_map/cond/branch_1_fun/ppermute | solution.py:446
  60.0 28.1 %collective-permute-start.26 = (f32[2432,128]{1,0:T(8,128)S(1)}, f32[2432,128]{1,0:T(8,128)}, u32[]{:S(2)}, u32[]{:S(2)}) collective-permute-start(f32[2432,128]{1,0:T(8,128)S(1)} %copy-done.26), channel_id=1, source_target_pairs={{0,1},{1,0},{2,3},{3,2},{4,5},{5,4},{6,7},{7,6},{8,9},{9,8},{10,11... | collective-permute-start | bytes 3735560 | tf_op jit(solution)/shard_map/cond/branch_1_fun/ppermute | solution.py:446
  109.9 31.7 %collective-permute-start.31 = (f32[1920,128]{1,0:T(8,128)}, f32[1920,128]{1,0:T(8,128)}, u32[]{:S(2)}, u32[]{:S(2)}) collective-permute-start(f32[1920,128]{1,0:T(8,128)} %get-tuple-element.352), channel_id=1, source_target_pairs={{0,3},{1,2},{2,1},{3,0},{4,7},{5,6},{6,5},{7,4},{8,11},{9,10},{10,... | collective-permute-start | bytes 2949128 | tf_op jit(solution)/shard_map/cond/branch_1_fun/ppermute | solution.py:446
  110.6 44.8 %collective-permute-start.30 = (f32[1920,128]{1,0:T(8,128)}, f32[1920,128]{1,0:T(8,128)}, u32[]{:S(2)}, u32[]{:S(2)}) collective-permute-start(f32[1920,128]{1,0:T(8,128)} %get-tuple-element.353), channel_id=1, source_target_pairs={{0,2},{1,3},{2,0},{3,1},{4,6},{5,7},{6,4},{7,5},{8,10},{9,11},{10,... | collective-permute-start | bytes 2949128 | tf_op jit(solution)/shard_map/cond/branch_1_fun/ppermute | solution.py:446
  112.0 43.3 %collective-permute-start.29 = (f32[1920,128]{1,0:T(8,128)}, f32[1920,128]{1,0:T(8,128)S(1)}, u32[]{:S(2)}, u32[]{:S(2)}) collective-permute-start(f32[1920,128]{1,0:T(8,128)} %get-tuple-element.354), channel_id=1, source_target_pairs={{0,1},{1,0},{2,3},{3,2},{4,5},{5,4},{6,7},{7,6},{8,9},{9,8},{10,11... | collective-permute-start | bytes 2949128 | tf_op jit(solution)/shard_map/cond/branch_1_fun/ppermute | solution.py:446
  196.1 24.0 %collective-permute-start.33 = (f32[128,1920]{1,0:T(8,128)S(1)}, f32[128,1920]{1,0:T(8,128)}, u32[]{:S(2)}, u32[]{:S(2)}) collective-permute-start(f32[128,1920]{1,0:T(8,128)S(1)} %dynamic-slice_bitcast_fusion.13), channel_id=1, source_target_pairs={{0,2},{1,3},{2,0},{3,1},{4,6},{5,7},{6,4},{7,5},{8,10},{9,11},{10,... | collective-permute-start | bytes 2949128 | tf_op jit(solution)/shard_map/cond/branch_1_fun/ppermute | solution.py:446
  228.0 39.7 %collective-permute-start.40 = (f32[256,128]{1,0:T(8,128)}, f32[256,128]{1,0:T(8,128)}, u32[]{:S(2)}, u32[]{:S(2)}) collective-permute-start(f32[256,128]{1,0:T(8,128)} %get-tuple-element.356), channel_id=1, source_target_pairs={{0,4},{4,8},{8,12},{12,0},{1,5},{5,9},{9,13},{13,1},{2,6},{6,10},{... | collective-permute-start | bytes 393224 | tf_op jit(solution)/shard_map/cond/branch_1_fun/ppermute | solution.py:418
  230.5 37.2 %collective-permute-start.42 = (f32[256,128]{1,0:T(8,128)}, f32[256,128]{1,0:T(8,128)}, u32[]{:S(2)}, u32[]{:S(2)}) collective-permute-start(f32[256,128]{1,0:T(8,128)} %get-tuple-element.357), channel_id=1, source_target_pairs={{0,12},{4,0},{8,4},{12,8},{1,13},{5,1},{9,5},{13,9},{2,14},{6,2},{... | collective-permute-start | bytes 393224 | tf_op jit(solution)/shard_map/cond/branch_1_fun/ppermute | solution.py:418
  230.5 40.0 %collective-permute-start.41 = (f32[256,128]{1,0:T(8,128)}, f32[256,128]{1,0:T(8,128)}, u32[]{:S(2)}, u32[]{:S(2)}) collective-permute-start(f32[256,128]{1,0:T(8,128)} %get-tuple-element.358), channel_id=1, source_target_pairs={{0,8},{4,12},{8,0},{12,4},{1,9},{5,13},{9,1},{13,5},{2,10},{6,14},... | collective-permute-start | bytes 393224 | tf_op jit(solution)/shard_map/cond/branch_1_fun/ppermute | solution.py:418
  232.0 69.4 %collective-permute-start.47 = (f32[128,1536]{1,0:T(8,128)}, f32[128,1536]{1,0:T(8,128)S(1)}, u32[]{:S(2)}, u32[]{:S(2)}) collective-permute-start(f32[128,1536]{1,0:T(8,128)} %reduce-scatter.8.cloned.1.call-done.packed), channel_id=1, source_target_pairs={{0,0},{1,4},{2,8},{3,12},{4,1},{5,5},{6,9},{7,13},{8,2},{9,6},{10,... | collective-permute-start | bytes 2359304 | tf_op jit(solution)/shard_map/cond/branch_1_fun/ppermute | solution.py:410
  272.2 27.7 %collective-permute-start.43 = (f32[128,128]{1,0:T(8,128)S(1)}, f32[128,128]{1,0:T(8,128)S(1)}, u32[]{:S(2)}, u32[]{:S(2)}) collective-permute-start(f32[128,128]{1,0:T(8,128)S(1)} %get-tuple-element.362), channel_id=1, source_target_pairs={{0,0},{1,4},{2,8},{3,12},{4,1},{5,5},{6,9},{7,13},{8,2},{9,6},{10,... | collective-permute-start | bytes 196616 | tf_op jit(solution)/shard_map/cond/branch_1_fun/ppermute | solution.py:410
  276.7 52.5 %collective-permute-start.51 = (f32[128,1920]{1,0:T(8,128)S(1)}, f32[128,1920]{1,0:T(8,128)S(1)}, u32[]{:S(2)}, u32[]{:S(2)}) collective-permute-start(f32[128,1920]{1,0:T(8,128)S(1)} %bitcast_add_fusion.5.image_rows), channel_id=1, source_target_pairs={{0,0},{1,4},{2,8},{3,12},{4,1},{5,5},{6,9},{7,13},{8,2},{9,6},{10,... | collective-permute-start | bytes 2949128 | tf_op jit(solution)/shard_map/cond/branch_1_fun/ppermute | solution.py:410
  299.8 8.1 %collective-permute-start.45 = (f32[128,128]{1,0:T(8,128)S(1)}, f32[128,128]{1,0:T(8,128)S(1)}, u32[]{:S(2)}, u32[]{:S(2)}) collective-permute-start(f32[128,128]{1,0:T(8,128)S(1)} %collective-permute-done.43), channel_id=1, source_target_pairs={{0,2},{1,3},{2,0},{3,1},{4,6},{5,7},{6,4},{7,5},{8,10},{9,11},{10,... | collective-permute-start | bytes 196616 | tf_op jit(solution)/shard_map/cond/branch_1_fun/ppermute | solution.py:446
  299.8 9.7 %collective-permute-start.44 = (f32[128,128]{1,0:T(8,128)S(1)}, f32[128,128]{1,0:T(8,128)S(1)}, u32[]{:S(2)}, u32[]{:S(2)}) collective-permute-start(f32[128,128]{1,0:T(8,128)S(1)} %collective-permute-done.43), channel_id=1, source_target_pairs={{0,1},{1,0},{2,3},{3,2},{4,5},{5,4},{6,7},{7,6},{8,9},{9,8},{10,11... | collective-permute-start | bytes 196616 | tf_op jit(solution)/shard_map/cond/branch_1_fun/ppermute | solution.py:446
  304.4 20.5 %collective-permute-start.48 = (f32[128,128]{1,0:T(8,128)S(1)}, f32[128,128]{1,0:T(8,128)S(1)}, u32[]{:S(2)}, u32[]{:S(2)}) collective-permute-start(f32[128,128]{1,0:T(8,128)S(1)} %get-tuple-element.359), channel_id=1, source_target_pairs={{0,4},{4,8},{8,12},{12,0},{1,5},{5,9},{9,13},{13,1},{2,6},{6,10},{... | collective-permute-start | bytes 196616 | tf_op jit(solution)/shard_map/cond/branch_1_fun/ppermute | solution.py:418
  308.0 17.0 %collective-permute-start.50 = (f32[128,128]{1,0:T(8,128)S(1)}, f32[128,128]{1,0:T(8,128)S(1)}, u32[]{:S(2)}, u32[]{:S(2)}) collective-permute-start(f32[128,128]{1,0:T(8,128)S(1)} %get-tuple-element.360), channel_id=1, source_target_pairs={{0,12},{4,0},{8,4},{12,8},{1,13},{5,1},{9,5},{13,9},{2,14},{6,2},{... | collective-permute-start | bytes 196616 | tf_op jit(solution)/shard_map/cond/branch_1_fun/ppermute | solution.py:418
  308.0 17.7 %collective-permute-start.49 = (f32[128,128]{1,0:T(8,128)S(1)}, f32[128,128]{1,0:T(8,128)S(1)}, u32[]{:S(2)}, u32[]{:S(2)}) collective-permute-start(f32[128,128]{1,0:T(8,128)S(1)} %get-tuple-element.361), channel_id=1, source_target_pairs={{0,8},{4,12},{8,0},{12,4},{1,9},{5,13},{9,1},{13,5},{2,10},{6,14},... | collective-permute-start | bytes 196616 | tf_op jit(solution)/shard_map/cond/branch_1_fun/ppermute | solution.py:418
  309.5 18.3 %collective-permute-start.46 = (f32[128,128]{1,0:T(8,128)S(1)}, f32[128,128]{1,0:T(8,128)S(1)}, u32[]{:S(2)}, u32[]{:S(2)}) collective-permute-start(f32[128,128]{1,0:T(8,128)S(1)} %collective-permute-done.45), channel_id=1, source_target_pairs={{0,1},{1,0},{2,3},{3,2},{4,5},{5,4},{6,7},{7,6},{8,9},{9,8},{10,11... | collective-permute-start | bytes 196616 | tf_op jit(solution)/shard_map/cond/branch_1_fun/ppermute | solution.py:446
  (12 other events, 179.2 us)
Sparse Core Ops, SparseCore 0:
  17.8 75.1 all-gather.12
  132.1 60.8 reduce-scatter.7
